TPU v7x, 256 devices: a whole 4x4x8 slice. The times are simulated.
256 devices in a mesh: gx: 16 (over z_hi, x), gy: 4 (over z_lo, core), gz: 4 (over y).
Axes of the slice: x: 4, y: 4, z: 8 (z_hi: 4, z_lo: 2; z = z_hi * 2 + z_lo), core: 2. Of those that a mesh axis runs over, the one named last changes fastest.
Arguments:
- density: float32 [256, 64, 512], P('gx', 'gy', 'gz'), may hold values from 0.8 to 1.2
- momentum: float32 [3, 256, 64, 512], P(None, 'gx', 'gy', 'gz'), may hold values from -1.5 to 1.5
- energy: float32 [256, 64, 512], P('gx', 'gy', 'gz'), may hold values from 2.5 to 3.5
- acoustic: float32 [4, 32, 16, 16, 512], P(None, 'gx', 'gy', 'gz'), may hold values from -3 to 3
- tile_slot: int32 [16, 4, 4, 8], P('gx', 'gy', 'gz'), may hold values from 0 to 63, as said below
- tile_element: int32 [16, 4, 4, 8], P('gx', 'gy', 'gz'), may hold values from 0 to 31
Outputs:
- density_next: float32 [256, 64, 512], P('gx', 'gy', 'gz')
- momentum_next: float32 [3, 256, 64, 512], P(None, 'gx', 'gy', 'gz')
- energy_next: float32 [256, 64, 512], P('gx', 'gy', 'gz')
- acoustic_next: float32 [4, 32, 16, 16, 512], P(None, 'gx', 'gy', 'gz')
Inputs may be any that keep to these rules, and one draw needn't show every extreme that they name: `tile_slot`: within one device's list the slots are distinct, so at most 4 tiles of one device go to any one device; every device sends exactly 4 of its 8 tiles to one device along gx; its other 4 tiles go to distinct slots of other devices.
All inputs are finite; a program needn't handle non-finite values.
Results may differ from a plain program's by a relative error of at most 0.0001.
Values sent between devices are 32-bit elements; how exact they have to be, the bound alone decides.
A program may use at most 128 MiB of HBM per device.

v0:
```python
import functools

import jax
import jax.numpy as jnp
import ml_dtypes
import numpy as np
from jax import lax
from jax.experimental import pallas as pl
from jax.experimental.pallas import tpu as pltpu
from jax.sharding import PartitionSpec as P

MESH = pl.DeviceIdType.MESH
F32 = jnp.float32
BF16 = jnp.bfloat16

flow_step = 0.05
viscosity = 0.2
sound_step = 0.02
lift_factor = 28.0
source_gain = 40.0
TILE_LANES = 1664


def derivative_numbers():
    order = 7
    points = np.array(
        [
            -1.0,
            -0.8717401485096066,
            -0.5917001814331423,
            -0.2092992179024789,
            0.2092992179024789,
            0.5917001814331423,
            0.8717401485096066,
            1.0,
        ]
    )
    previous = np.ones(8)
    current = points * 1.0
    for degree in range(1, order):
        following = ((2 * degree + 1) * points * current - degree * previous) / (degree + 1)
        previous = current
        current = following
    table = np.zeros((8, 8))
    for row in range(8):
        for column in range(8):
            if row != column:
                table[row, column] = current[row] / (
                    current[column] * (points[row] - points[column])
                )
    table[0, 0] = -order * (order + 1) / 4.0
    table[order, order] = order * (order + 1) / 4.0
    return table


def split_table(table):
    table = table.astype(np.float32)
    high = table.astype(ml_dtypes.bfloat16)
    low = (table - high.astype(np.float32)).astype(ml_dtypes.bfloat16)
    return high, low


def tables():
    table = derivative_numbers()
    eye = np.eye(8)
    along_x = np.kron(np.kron(table, eye), eye).T
    along_y = np.kron(np.kron(np.eye(4), table), eye).T
    along_z = np.kron(np.kron(np.eye(4), eye), table).T
    order = np.zeros((512, 512), ml_dtypes.bfloat16)
    for c in range(8):
        for ab in range(64):
            order[c * 64 + ab, ab * 8 + c] = 1.0
    return (*split_table(along_x), *split_table(along_y), *split_table(along_z), order)


def iota(shape, dim):
    return lax.broadcasted_iota(jnp.int32, shape, dim)


def fluxes(state):
    rho, mx, my, mz, energy = state
    inverse = 1.0 / rho
    vx, vy, vz = mx * inverse, my * inverse, mz * inverse
    pressure = 0.4 * (energy - 0.5 * (mx * vx + my * vy + mz * vz))
    total = energy + pressure
    xy, xz, yz = mx * vy, mx * vz, my * vz
    return (
        [mx, mx * vx + pressure, xy, xz, total * vx],
        [my, xy, my * vy + pressure, yz, total * vy],
        [mz, xz, yz, mz * vz + pressure, total * vz],
    )


def halves(value):
    high = value.astype(BF16).astype(F32)
    return high, value - high


def kernel(
    zh_count, x_count, gy_count, gz_count,
    rho_hbm, mom_hbm, energy_hbm, sound_hbm, slot_ref, element_ref,
    dxh_hbm, dxl_hbm, dyh_hbm, dyl_hbm, dzh_hbm, dzl_hbm, order_hbm,
    rho_out, mom_out, energy_out, sound_out,
    s0, s1, s2, vel, vort, mref, fref, tiles,
    hx, hy, hz, sy, sz, ax, ay, az, axs, ays, azs,
    stage, q0, q1, n0, chars, near,
    dxh, dxl, dyh, dyl, dzh, dzl, order,
    in_sem, out_sem, flow_send, flow_recv, face_send, face_recv, tile_send, tile_recv,
):
    gx, gy, gz = lax.axis_index("gx"), lax.axis_index("gy"), lax.axis_index("gz")
    gx_count = zh_count * x_count
    zh, xi = gx // x_count, lax.rem(gx, x_count)

    def at_x(step):
        return (lax.rem(gx + step + gx_count, gx_count), gy, gz)

    def at_y(step):
        return (gx, lax.rem(gy + step + gy_count, gy_count), gz)

    def at_z(step):
        return (gx, gy, lax.rem(gz + step + gz_count, gz_count))

    def at_zh(step):
        return (lax.rem(zh + step, zh_count) * x_count + xi, gy, gz)

    def at_xi(step):
        return (zh * x_count + lax.rem(xi + step, x_count), gy, gz)

    loads = [
        (rho_hbm, s0.at[0]), (mom_hbm, s0.at[1:4]), (energy_hbm, s0.at[4]), (sound_hbm, stage),
        (order_hbm, order), (dxh_hbm, dxh), (dxl_hbm, dxl), (dyh_hbm, dyh), (dyl_hbm, dyl),
        (dzh_hbm, dzh), (dzl_hbm, dzl),
    ]
    loads = [pltpu.make_async_copy(a, b, in_sem.at[i]) for i, (a, b) in enumerate(loads)]
    for load in loads:
        load.start()

    barrier = pltpu.get_barrier_semaphore()
    partners = [at_x(-1), at_x(1), at_y(-1), at_y(1), at_z(-1), at_z(1)]
    partners += [at_zh(k) for k in range(1, zh_count)] + [at_xi(j) for j in range(1, x_count)]
    for partner in partners:
        pl.semaphore_signal(barrier, inc=1, device_id=partner, device_id_type=MESH)

    lane = iota((16, 128), 1)
    row = iota((16, 128), 0)
    odd = lax.rem(lane, 2) == 1
    edge = (lane == 0) | (lane == 127)
    pair = lane // 2

    pending = []

    def send(src, dst, send_sem, recv_sem, device):
        copy = pltpu.make_async_remote_copy(
            src_ref=src, dst_ref=dst, send_sem=send_sem, recv_sem=recv_sem,
            device_id=device, device_id_type=MESH,
        )
        copy.start()
        pending.append(copy)
        return copy

    def flow_sends(turn, x_source, comps):
        def go(i, src, dst, device):
            return send(src, dst, flow_send.at[turn, i], flow_recv.at[turn, i], device)

        return [
            go(0, x_source(240), hx.at[turn, 0, comps], at_x(1)),
            go(1, x_source(0), hx.at[turn, 1, comps], at_x(-1)),
            go(2, sy.at[turn, 0, comps], hy.at[turn, 0, comps], at_y(1)),
            go(3, sy.at[turn, 1, comps], hy.at[turn, 1, comps], at_y(-1)),
            go(4, sz.at[turn, comps], hz.at[turn, 0, comps], at_z(1)),
            go(5, sz.at[turn, comps], hz.at[turn, 1, comps], at_z(-1)),
        ]

    def slab(x):
        return pl.ds(pl.multiple_of(x * 16, 16), 16)

    def pack_lanes(packed, values, x):
        here = pair == x
        return [jnp.where(here, pltpu.roll(v, 2 * x + 1, 1), p) for p, v in zip(packed, values)]

    def pack_rows(turn, ref, comps):
        for c in comps:
            sy[turn, 0, c] = ref[c, pl.ds(15, 16, stride=16), :]
            sy[turn, 1, c] = ref[c, pl.ds(0, 16, stride=16), :]

    for load in loads[:3]:
        load.wait()
    pack_rows(0, s0, range(5))

    def pack_first(x, packed):
        return pack_lanes(packed, [s0[c, slab(x), :] for c in range(5)], x)

    first_slab = [s0[c, 0:16, :] for c in range(5)]
    for c, value in enumerate(lax.fori_loop(0, 16, pack_first, first_slab)):
        sz[0, c] = value
    pl.semaphore_wait(barrier, len(partners))
    every = pl.ds(0, 5)
    round_0 = flow_sends(0, lambda r: s0.at[:, r : r + 16, :], every)

    def face_sends(turn, q):
        for d in range(3):
            for j in range(4):
                block = slice(128 * j, 128 * j + 128)
                chars[0, d, j] = q[0, :, block] - q[1 + d, :, block]
                chars[1, d, j] = q[0, :, block] + q[1 + d, :, block]
        axs[turn, 0] = chars[0, 0, 0, 0:16, :]
        axs[turn, 1] = chars[1, 0, 3, 16:32, :]
        for side, top in ((0, 0), (1, 12)):
            for j in range(4):
                block = slice(128 * j, 128 * j + 128)
                ays[turn, side, 0:4, block] = chars[side, 1, j, top : top + 4, :]
                ays[turn, side, 4:8, block] = chars[side, 1, j, top + 16 : top + 20, :]
                azs[turn, side, :, block] = chars[side, 2, j, pl.ds(3 * side, 8, stride=4), :]

        def go(i, src, dst, device):
            return send(src, dst, face_send.at[turn, i], face_recv.at[turn, i], device)

        return [
            go(0, axs.at[turn, 0], ax.at[turn, 0], at_x(-1)),
            go(1, axs.at[turn, 1], ax.at[turn, 1], at_x(1)),
            go(2, ays.at[turn, 0], ay.at[turn, 0], at_y(-1)),
            go(3, ays.at[turn, 1], ay.at[turn, 1], at_y(1)),
            go(4, azs.at[turn, 0], az.at[turn, 0], at_z(-1)),
            go(5, azs.at[turn, 1], az.at[turn, 1], at_z(1)),
        ]

    def apply3(value, high, low):
        rows = value.shape[0]
        top, rest = halves(value)
        both = jnp.concatenate([top, rest], axis=0).astype(BF16)
        part = jnp.dot(both, high, preferred_element_type=F32)
        return (
            part[:rows] + part[rows:]
            + jnp.dot(top.astype(BF16), low, preferred_element_type=F32)
        )

    def derivative(d, value):
        if d == 0:
            return apply3(value, dxh[...], dxl[...])
        high, low = (dyh, dyl) if d == 1 else (dzh, dzl)
        split = [apply3(value[:, s : s + 256], high[...], low[...]) for s in (0, 256)]
        return jnp.concatenate(split, axis=1)

    lane32 = iota((32, 128), 1)

    def rates(q, out, gain, base, copies, turn, with_pressure):
        total = None
        for d in range(3):
            if with_pressure:
                both = derivative(d, jnp.concatenate([q[0], q[1 + d]], axis=0))
                out[1 + d] = base(1 + d) - gain * both[:32]
                both = both[32:]
            else:
                both = derivative(d, q[1 + d])
                out[1 + d] = base(1 + d)
            total = both if total is None else total + both
        out[0] = base(0) - gain * total
        for side, d, move in ((0, 1, 28), (1, 1, 4), (0, 2, 31), (1, 2, 1)):
            for j in range(4):
                near[side, d - 1, j] = pltpu.roll(chars[side, d, j], move, 0)
        for copy in copies:
            copy.wait_recv()
        for side, top in ((0, 12), (1, 0)):
            for j in range(4):
                block = slice(128 * j, 128 * j + 128)
                near[side, 0, j, top : top + 4, :] = ay[turn, side, 0:4, block]
                near[side, 0, j, top + 16 : top + 20, :] = ay[turn, side, 4:8, block]
                near[side, 1, j, pl.ds(3 - 3 * side, 8, stride=4), :] = az[turn, side, :, block]
        k = 0.5 * lift_factor * gain
        other = jnp.concatenate([chars[0, 0, 0, 16:32, :], ax[turn, 0]], axis=0)
        jump = pltpu.roll(other, 64, 1) - chars[0, 0, 3]
        jump = jnp.where(lane32 >= 64, k * jump, 0.0)
        out[0, :, 384:512] += jump
        out[1, :, 384:512] -= jump
        other = jnp.concatenate([ax[turn, 1], chars[1, 0, 3, 0:16, :]], axis=0)
        jump = chars[1, 0, 0] - pltpu.roll(other, 64, 1)
        jump = jnp.where(lane32 < 64, k * jump, 0.0)
        out[0, :, 0:128] -= jump
        out[1, :, 0:128] -= jump
        for d, period, move in ((1, 64, 56), (2, 8, 7)):
            place = lax.rem(lane32, period)
            span = period - move
            for j in range(4):
                block = slice(128 * j, 128 * j + 128)
                high = pltpu.roll(near[0, d - 1, j], move, 1) - chars[0, d, j]
                high = jnp.where(place >= move, k * high, 0.0)
                low = chars[1, d, j] - pltpu.roll(near[1, d - 1, j], 128 - move, 1)
                low = jnp.where(place < span, k * low, 0.0)
                out[0, :, block] += high - low
                out[1 + d, :, block] -= high + low

    loads[3].wait()
    for i in range(32):
        c, part = i // 8, i % 8
        q0[c, 4 * part : 4 * part + 4, :] = stage[i]
    faces_0 = face_sends(0, q0)

    def interior(source, target, gain, base):
        half, visc = 0.5 * gain, viscosity * gain

        def update(x, before, first):
            state = [source[c, slab(x), :] for c in range(5)]
            along_x, along_y, along_z = fluxes(state)
            sums, later = [], []
            for c in range(5):
                soft = visc * state[c]
                acc = base(c, x, state[c]) - 6.0 * soft
                part = half * along_z[c]
                acc += pltpu.roll(jnp.where(lane == 0, 0.0, soft - part), 127, 1)
                acc += pltpu.roll(jnp.where(lane == 127, 0.0, soft + part), 1, 1)
                part = half * along_y[c]
                acc += pltpu.roll(jnp.where(row == 0, 0.0, soft - part), 15, 0)
                acc += pltpu.roll(jnp.where(row == 15, 0.0, soft + part), 1, 0)
                part = half * along_x[c]
                if not first:
                    target[c, slab(x - 1), :] = before[c] + (soft - part)
                    acc += before[5 + c]
                sums.append(acc)
                later.append(soft + part)
            return sums + later

        carry = update(0, None, True)
        carry = lax.fori_loop(1, 16, lambda x, b: update(x, b, False), carry)
        for c in range(5):
            target[c, 240:256, :] = carry[c]

    def boundary(turn, target, gain, copies):
        half, visc = 0.5 * gain, viscosity * gain
        for copy in copies:
            copy.wait_recv()
        lower, upper = [hx[turn, 0, c] for c in range(5)], [hx[turn, 1, c] for c in range(5)]
        low_flux, up_flux = fluxes(lower)[0], fluxes(upper)[0]
        for c in range(5):
            target[c, 0:16, :] += visc * lower[c] + half * low_flux[c]
            target[c, 240:256, :] += visc * upper[c] - half * up_flux[c]
        lower, upper = [hy[turn, 0, c] for c in range(5)], [hy[turn, 1, c] for c in range(5)]
        low_flux, up_flux = fluxes(lower)[1], fluxes(upper)[1]
        for c in range(5):
            target[c, pl.ds(0, 16, stride=16), :] += visc * lower[c] + half * low_flux[c]
            target[c, pl.ds(15, 16, stride=16), :] += visc * upper[c] - half * up_flux[c]
        both = [
            jnp.where(odd, pltpu.roll(hz[turn, 0, c], 1, 1), pltpu.roll(hz[turn, 1, c], 127, 1))
            for c in range(5)
        ]
        flux = fluxes(both)[2]
        return [
            visc * both[c] + jnp.where(odd, half * flux[c], -half * flux[c]) for c in range(5)
        ]

    def add_edges(target, terms, x):
        values = []
        for c in range(5):
            moved = pltpu.roll(terms[c], 127 - 2 * x, 1)
            value = target[c, slab(x), :] + jnp.where(edge, moved, 0.0)
            target[c, slab(x), :] = value
            values.append(value)
        return values

    interior(s0, s1, flow_step, lambda c, x, u: u)
    terms = boundary(0, s1, flow_step, round_0)
    pack_first_slab = [s1[c, 0:16, :] for c in range(5)]

    def finish_first(x, packed):
        return pack_lanes(packed, add_edges(s1, terms, x), x)

    packed = lax.fori_loop(0, 16, finish_first, pack_first_slab)
    for c in range(5):
        sz[1, c] = packed[c]
    pack_rows(1, s1, range(5))
    round_1 = flow_sends(1, lambda r: s1.at[:, r : r + 16, :], every)

    interior(s1, s2, 0.5 * flow_step, lambda c, x, u: 0.5 * (s0[c, slab(x), :] + u))
    terms_2 = boundary(1, s2, 0.5 * flow_step, round_1)

    def finish_second(x, packed):
        values = add_edges(s2, terms_2, x)
        inverse = 1.0 / values[0]
        vx, vy, vz = (values[d] * inverse for d in (1, 2, 3))
        vel[0, slab(x), :], vel[1, slab(x), :], vel[2, slab(x), :] = vy, vz, vx
        return pack_lanes(packed, [vy, vx], x)

    zero = jnp.zeros((16, 128), F32)
    packed = lax.fori_loop(0, 16, finish_second, [zero, zero])
    sz[2, 0], sz[2, 1] = packed
    for i, comp in enumerate((1, 2)):
        sy[2, 0, i] = vel[comp, pl.ds(15, 16, stride=16), :]
        sy[2, 1, i] = vel[comp, pl.ds(0, 16, stride=16), :]
    round_2 = flow_sends(2, lambda r: vel.at[0:2, r : r + 16, :], pl.ds(0, 2))

    stores = [
        pltpu.make_async_copy(s2.at[0], rho_out, out_sem.at[0]),
        pltpu.make_async_copy(s2.at[1:4], mom_out, out_sem.at[1]),
        pltpu.make_async_copy(s2.at[4], energy_out, out_sem.at[2]),
    ]
    for store in stores:
        store.start()

    def dy(f):
        up = pltpu.roll(jnp.where(row == 0, 0.0, f), 15, 0)
        return up - pltpu.roll(jnp.where(row == 15, 0.0, f), 1, 0)

    def dz(f):
        up = pltpu.roll(jnp.where(lane == 0, 0.0, f), 127, 1)
        return up - pltpu.roll(jnp.where(lane == 127, 0.0, f), 1, 1)

    def curl(x, carry):
        vy, vz, vx = (vel[i, slab(x), :] for i in range(3))
        after = slab(jnp.minimum(x + 1, 15))
        before = slab(jnp.maximum(x - 1, 0))
        dx_vy, dx_vz = (
            jnp.where(x < 15, vel[i, after, :], 0.0) - jnp.where(x > 0, vel[i, before, :], 0.0)
            for i in range(2)
        )
        vort[0, slab(x), :] = dy(vz) - dz(vy)
        vort[1, slab(x), :] = dz(vx) - dx_vz
        vort[2, slab(x), :] = dx_vy - dy(vx)
        return carry

    lax.fori_loop(0, 16, curl, 0)
    for copy in round_2:
        copy.wait_recv()
    vort[1, 0:16, :] += hx[2, 0, 1]
    vort[2, 0:16, :] -= hx[2, 0, 0]
    vort[1, 240:256, :] -= hx[2, 1, 1]
    vort[2, 240:256, :] += hx[2, 1, 0]
    vort[0, pl.ds(0, 16, stride=16), :] -= hy[2, 0, 0]
    vort[2, pl.ds(0, 16, stride=16), :] += hy[2, 0, 1]
    vort[0, pl.ds(15, 16, stride=16), :] += hy[2, 1, 0]
    vort[2, pl.ds(15, 16, stride=16), :] -= hy[2, 1, 1]
    side_y, side_x = (
        jnp.where(odd, pltpu.roll(hz[2, 0, i], 1, 1), pltpu.roll(hz[2, 1, i], 127, 1))
        for i in range(2)
    )
    side_y = jnp.where(odd, side_y, -side_y)
    side_x = jnp.where(odd, -side_x, side_x)

    def lamb_pair(a, carry):
        sums = [None] * 3
        for x in (2 * a, 2 * a + 1):
            wx = vort[0, slab(x), :] + jnp.where(edge, pltpu.roll(side_y, 127 - 2 * x, 1), 0.0)
            wy = vort[1, slab(x), :] + jnp.where(edge, pltpu.roll(side_x, 127 - 2 * x, 1), 0.0)
            wz = vort[2, slab(x), :]
            vy, vz, vx = (vel[i, slab(x), :] for i in range(3))
            parts = (wy * vz - wz * vy, wz * vx - wx * vz, wx * vy - wy * vx)
            sums = [p if s is None else s + p for s, p in zip(sums, parts)]
        for d in range(3):
            mref[d, slab(a), :] = 0.0625 * sums[d]
        return carry

    lax.fori_loop(0, 8, lamb_pair, 0)
    coarse = [
        mref[d, pl.ds(0, 64, stride=2), :] + mref[d, pl.ds(1, 64, stride=2), :] for d in range(3)
    ]
    fref[0] = jnp.transpose(jnp.concatenate([coarse[0], coarse[1]], axis=0))
    fref[1] = jnp.transpose(jnp.concatenate([coarse[2], coarse[2]], axis=0))
    pieces = [
        [
            fref[i, pl.ds(2 * c, 8, stride=16), :] + fref[i, pl.ds(2 * c + 1, 8, stride=16), :]
            for c in range(8)
        ]
        for i in range(2)
    ]
    left = iota((8, 128), 1) < 64
    rows = [[], [], []]
    for j in range(4):
        a, b = pieces[0][2 * j], pieces[0][2 * j + 1]
        rows[0].append(jnp.where(left, a, pltpu.roll(b, 64, 1)))
        rows[1].append(jnp.where(left, pltpu.roll(a, 64, 1), b))
        rows[2].append(jnp.where(left, pieces[1][2 * j], pieces[1][2 * j + 1]))
    own = jnp.concatenate([jnp.concatenate(r, axis=1) for r in rows], axis=0)
    high, rest = halves(own)
    middle, low = halves(rest)
    loads[4].wait()
    parts = jnp.concatenate([high, middle, low], axis=0).astype(BF16)
    parts = jnp.dot(parts, order[...], preferred_element_type=F32)
    own = parts[0:24] + parts[24:48] + parts[48:72]
    for d in range(3):
        tiles[gx, :, 512 * d : 512 * d + 512] = own[8 * d : 8 * d + 8]
    row8 = iota((8, 128), 0)
    target = jnp.zeros((8, 128), jnp.int32)
    for t in range(8):
        address = lax.div(slot_ref[0, 0, 0, t], 4) * 32 + element_ref[0, 0, 0, t]
        target = jnp.where(row8 == t, address, target)
    tiles[gx, :, 1536:1664] = target.astype(F32)

    def tile_copy(i, source, device):
        return send(tiles.at[source], tiles.at[source], tile_send.at[i], tile_recv.at[i], device)

    down = [tile_copy(k - 1, gx, at_zh(k)) for k in range(1, zh_count)]
    across = []

    def pass_on(k):
        source = lax.rem(zh - k + zh_count, zh_count) * x_count + xi
        for j in range(1, x_count):
            i = zh_count - 1 + k * (x_count - 1) + j - 1
            across.append(tile_copy(i, source, at_xi(j)))

    pass_on(0)

    for load in loads[5:]:
        load.wait()
    rates(q0, q1, sound_step, lambda c: q0[c], faces_0, 0, True)
    for k in range(1, zh_count):
        down[k - 1].wait_recv()
        pass_on(k)
    faces_1 = face_sends(1, q1)
    rates(q1, n0, 0.5 * sound_step, lambda c: 0.5 * (q0[c] + q1[c]), faces_1, 1, True)

    for copy in across:
        copy.wait_recv()
    gx_tiles = 8 * gx_count
    address = tiles[:, :, 1536:1664].reshape(gx_tiles, 128)
    wanted = (gx * 32 + iota((gx_tiles, 128), 1)).astype(F32)
    picking = jnp.where(address == wanted, 1.0, 0.0)
    picking = jnp.transpose(picking)[0:32].astype(BF16)
    for d in range(3):
        block = tiles[:, :, 512 * d : 512 * d + 512].reshape(gx_tiles, 512)
        high, low = halves(block)
        both = jnp.dot(picking, high.astype(BF16), preferred_element_type=F32)
        both += jnp.dot(picking, low.astype(BF16), preferred_element_type=F32)
        q1[1 + d] = -source_gain * sound_step * both
    q1[0] = jnp.zeros((32, 512), F32)
    faces_2 = face_sends(2, q1)
    rates(q1, q0, 0.5 * sound_step, lambda c: n0[c] + q1[c], faces_2, 2, False)
    for i in range(32):
        c, part = i // 8, i % 8
        stage[i] = q0[c, 4 * part : 4 * part + 4, :]
    stores.append(pltpu.make_async_copy(stage, sound_out, out_sem.at[3]))
    stores[-1].start()
    for copy in pending:
        copy.wait_send()
    for store in stores:
        store.wait()


def solution(mesh):
    gx_count, gy_count, gz_count = (mesh.shape[a] for a in ("gx", "gy", "gz"))
    x_count = 4 if gx_count == 16 else 2
    zh_count = gx_count // x_count
    tile_sends = (zh_count - 1) + zh_count * (x_count - 1)
    consts = tables()

    def on_device(density, momentum, energy, acoustic, tile_slot, tile_element):
        anywhere = pl.BlockSpec(memory_space=pl.ANY)
        scalars = pl.BlockSpec(memory_space=pltpu.SMEM)
        out_shape = (
            jax.ShapeDtypeStruct((256, 128), F32),
            jax.ShapeDtypeStruct((3, 256, 128), F32),
            jax.ShapeDtypeStruct((256, 128), F32),
            jax.ShapeDtypeStruct((32, 4, 512), F32),
        )
        vmem = pltpu.VMEM
        scratch = [
            vmem((5, 256, 128), F32), vmem((5, 256, 128), F32), vmem((5, 256, 128), F32),
            vmem((3, 256, 128), F32), vmem((3, 256, 128), F32), vmem((3, 128, 128), F32),
            vmem((2, 128, 128), F32), vmem((gx_count, 8, TILE_LANES), F32),
            vmem((3, 2, 5, 16, 128), F32), vmem((3, 2, 5, 16, 128), F32),
            vmem((3, 2, 5, 16, 128), F32), vmem((3, 2, 5, 16, 128), F32),
            vmem((3, 5, 16, 128), F32),
            vmem((3, 2, 16, 128), F32), vmem((3, 2, 8, 512), F32), vmem((3, 2, 8, 512), F32),
            vmem((3, 2, 16, 128), F32), vmem((3, 2, 8, 512), F32), vmem((3, 2, 8, 512), F32),
            vmem((32, 4, 512), F32), vmem((4, 32, 512), F32), vmem((4, 32, 512), F32),
            vmem((4, 32, 512), F32), vmem((2, 3, 4, 32, 128), F32), vmem((2, 2, 4, 32, 128), F32),
            vmem((512, 512), BF16), vmem((512, 512), BF16), vmem((256, 256), BF16),
            vmem((256, 256), BF16), vmem((256, 256), BF16), vmem((256, 256), BF16),
            vmem((512, 512), BF16),
            pltpu.SemaphoreType.DMA((11,)), pltpu.SemaphoreType.DMA((4,)),
            pltpu.SemaphoreType.DMA((3, 6)), pltpu.SemaphoreType.DMA((3, 6)),
            pltpu.SemaphoreType.DMA((3, 6)), pltpu.SemaphoreType.DMA((3, 6)),
            pltpu.SemaphoreType.DMA((tile_sends,)), pltpu.SemaphoreType.DMA((tile_sends,)),
        ]
        outs = pl.pallas_call(
            functools.partial(kernel, zh_count, x_count, gy_count, gz_count),
            out_shape=out_shape,
            in_specs=[anywhere] * 4 + [scalars] * 2 + [anywhere] * 7,
            out_specs=[anywhere] * 4,
            scratch_shapes=scratch,
            compiler_params=pltpu.CompilerParams(
                collective_id=0, has_side_effects=True, vmem_limit_bytes=60 * 2**20
            ),
            cost_estimate=pl.CostEstimate(
                flops=10**9, bytes_accessed=4 * 2**20, transcendentals=0
            ),
        )(
            density.reshape(256, 128), momentum.reshape(3, 256, 128), energy.reshape(256, 128),
            acoustic.reshape(32, 4, 512), tile_slot, tile_element,
            *[jnp.asarray(c) for c in consts],
        )
        return (
            outs[0].reshape(16, 16, 128), outs[1].reshape(3, 16, 16, 128),
            outs[2].reshape(16, 16, 128), outs[3].reshape(4, 2, 4, 4, 512),
        )

    in_specs = (
        P("gx", "gy", "gz"), P(None, "gx", "gy", "gz"), P("gx", "gy", "gz"),
        P(None, "gx", "gy", "gz", None), P("gx", "gy", "gz", None), P("gx", "gy", "gz", None),
    )
    out_specs = (
        P("gx", "gy", "gz"), P(None, "gx", "gy", "gz"), P("gx", "gy", "gz"),
        P(None, "gx", "gy", "gz", None),
    )
    return jax.shard_map(
        on_device, mesh=mesh, in_specs=in_specs, out_specs=out_specs, check_vma=False
    )
```

profile of v0, /device:TPU:2, one launch (start us, length us, event | category | flops | bytes accessed | tf_op | source)
XLA Modules:
  0.0 55.1 jit_solution(5717011122847259370)
XLA Ops:
  0.6 49.4 %shard_map.156 = (f32[256,128]{1,0:T(8,128)}, f32[3,256,128]{2,1,0:T(8,128)}, f32[256,128]{1,0:T(8,128)}, f32[32,4,512]{2,1,0:T(4,128)}) custom-call(f32[256,128]{1,0:T(8,128)} %bitcast.14, f32[3,256,128]{2,1,0:T(8,128)} %bitcast.12, f32[256,128]{1,0:T(8,128)} %bitcast.15, f32[32,4,512]{2,1,0:T(4,128)} %bitcast.13, s32[1,1,1,8]{3,2,1,0:T(1,128)} %slot_ref.1, ...), custom_call_target="tpu_custom_call" | custom-call | flops 1000000000 | bytes 4194304 | tf_op jit(solution)/shard_map/pallas_call | solution.py:572
  50.0 1.6 %copy.21 = f32[16,16,128]{2,1,0:T(8,128)} copy(f32[16,16,128]{2,1,0:T(8,128)} %bitcast.11) | data formatting | bytes 262144
  51.6 0.0 copy-start.1
  51.6 1.8 %copy.22 = f32[3,16,16,128]{3,2,1,0:T(8,128)} copy(f32[3,16,16,128]{3,2,1,0:T(8,128)} %bitcast.8) | data formatting | bytes 786432
  53.4 0.0 copy-done.1
  53.4 0.0 copy-start
  53.4 0.7 %copy.23 = f32[16,16,128]{2,1,0:T(8,128)} copy(f32[16,16,128]{2,1,0:T(8,128)S(1)} %bitcast.10) | data formatting | bytes 262144
  54.0 0.3 copy-done
  54.4 0.7 %copy.24 = f32[4,2,4,4,512]{4,3,2,1,0:T(4,128)} copy(f32[4,2,4,4,512]{4,3,2,1,0:T(4,128)S(1)} %bitcast.9) | data formatting | bytes 524288
Async XLA Ops:
  51.6 1.8 %copy-start.1 = (f32[256,128]{1,0:T(8,128)S(1)}, f32[256,128]{1,0:T(8,128)}, u32[]{:S(2)}) copy-start(f32[256,128]{1,0:T(8,128)} %get-tuple-element.10) | copy-start | bytes 393220
  53.4 1.0 %copy-start = (f32[32,4,512]{2,1,0:T(4,128)S(1)}, f32[32,4,512]{2,1,0:T(4,128)}, u32[]{:S(2)}) copy-start(f32[32,4,512]{2,1,0:T(4,128)} %get-tuple-element.11) | copy-start | bytes 786436
where the time goes:
time: 55.6 us; the launch traced here: 55.1 us
  Pallas kernels  49.4 us (89%)
  local copies, waits for them, and re-layouts  5.07 us (9%)
  between operations  0.64 us (1%)
    pallas_call x1, Pallas kernels, on_device(): pl.pallas_call(functools.partial(kernel, zh_count, x_count, gy_count, gz_...  49.4 us
    unnamed x8, local copies, waits for them, and re-layouts  5.07 us

commit v1 on v0

--- a/solution.py
+++ b/solution.py
@@ -126,6 +126,12 @@
     def at_xi(step):
         return (zh * x_count + lax.rem(xi + step, x_count), gy, gz)
 
+    barrier = pltpu.get_barrier_semaphore()
+    partners = [at_x(-1), at_x(1), at_y(-1), at_y(1), at_z(-1), at_z(1)]
+    partners += [at_zh(k) for k in range(1, zh_count)] + [at_xi(j) for j in range(1, x_count)]
+    for partner in partners:
+        pl.semaphore_signal(barrier, inc=1, device_id=partner, device_id_type=MESH)
+
     loads = [
         (rho_hbm, s0.at[0]), (mom_hbm, s0.at[1:4]), (energy_hbm, s0.at[4]), (sound_hbm, stage),
         (order_hbm, order), (dxh_hbm, dxh), (dxl_hbm, dxl), (dyh_hbm, dyh), (dyl_hbm, dyl),
@@ -135,12 +141,6 @@
     for load in loads:
         load.start()
 
-    barrier = pltpu.get_barrier_semaphore()
-    partners = [at_x(-1), at_x(1), at_y(-1), at_y(1), at_z(-1), at_z(1)]
-    partners += [at_zh(k) for k in range(1, zh_count)] + [at_xi(j) for j in range(1, x_count)]
-    for partner in partners:
-        pl.semaphore_signal(barrier, inc=1, device_id=partner, device_id_type=MESH)
-
     lane = iota((16, 128), 1)
     row = iota((16, 128), 0)
     odd = lax.rem(lane, 2) == 1
@@ -158,17 +158,21 @@
         pending.append(copy)
         return copy
 
-    def flow_sends(turn, x_source, comps):
-        def go(i, src, dst, device):
-            return send(src, dst, flow_send.at[turn, i], flow_recv.at[turn, i], device)
-
+    def flow_go(turn, i, src, dst, device):
+        return send(src, dst, flow_send.at[turn, i], flow_recv.at[turn, i], device)
+
+    def sends_x(turn, x_source, comps):
         return [
-            go(0, x_source(240), hx.at[turn, 0, comps], at_x(1)),
-            go(1, x_source(0), hx.at[turn, 1, comps], at_x(-1)),
-            go(2, sy.at[turn, 0, comps], hy.at[turn, 0, comps], at_y(1)),
-            go(3, sy.at[turn, 1, comps], hy.at[turn, 1, comps], at_y(-1)),
-            go(4, sz.at[turn, comps], hz.at[turn, 0, comps], at_z(1)),
-            go(5, sz.at[turn, comps], hz.at[turn, 1, comps], at_z(-1)),
+            flow_go(turn, 0, x_source(240), hx.at[turn, 0, comps], at_x(1)),
+            flow_go(turn, 1, x_source(0), hx.at[turn, 1, comps], at_x(-1)),
+        ]
+
+    def sends_yz(turn, comps):
+        return [
+            flow_go(turn, 2, sz.at[turn, comps], hz.at[turn, 0, comps], at_z(1)),
+            flow_go(turn, 3, sz.at[turn, comps], hz.at[turn, 1, comps], at_z(-1)),
+            flow_go(turn, 4, sy.at[turn, 0, comps], hy.at[turn, 0, comps], at_y(1)),
+            flow_go(turn, 5, sy.at[turn, 1, comps], hy.at[turn, 1, comps], at_y(-1)),
         ]
 
     def slab(x):
@@ -195,7 +199,8 @@
         sz[0, c] = value
     pl.semaphore_wait(barrier, len(partners))
     every = pl.ds(0, 5)
-    round_0 = flow_sends(0, lambda r: s0.at[:, r : r + 16, :], every)
+    round_x = sends_x(0, lambda r: s0.at[:, r : r + 16, :], every)
+    round_yz = sends_yz(0, every)
 
     def face_sends(turn, q):
         for d in range(3):
@@ -258,7 +263,7 @@
         for side, d, move in ((0, 1, 28), (1, 1, 4), (0, 2, 31), (1, 2, 1)):
             for j in range(4):
                 near[side, d - 1, j] = pltpu.roll(chars[side, d, j], move, 0)
-        for copy in copies:
+        for copy in copies[2:6]:
             copy.wait_recv()
         for side, top in ((0, 12), (1, 0)):
             for j in range(4):
@@ -267,16 +272,6 @@
                 near[side, 0, j, top + 16 : top + 20, :] = ay[turn, side, 4:8, block]
                 near[side, 1, j, pl.ds(3 - 3 * side, 8, stride=4), :] = az[turn, side, :, block]
         k = 0.5 * lift_factor * gain
-        other = jnp.concatenate([chars[0, 0, 0, 16:32, :], ax[turn, 0]], axis=0)
-        jump = pltpu.roll(other, 64, 1) - chars[0, 0, 3]
-        jump = jnp.where(lane32 >= 64, k * jump, 0.0)
-        out[0, :, 384:512] += jump
-        out[1, :, 384:512] -= jump
-        other = jnp.concatenate([ax[turn, 1], chars[1, 0, 3, 0:16, :]], axis=0)
-        jump = chars[1, 0, 0] - pltpu.roll(other, 64, 1)
-        jump = jnp.where(lane32 < 64, k * jump, 0.0)
-        out[0, :, 0:128] -= jump
-        out[1, :, 0:128] -= jump
         for d, period, move in ((1, 64, 56), (2, 8, 7)):
             place = lax.rem(lane32, period)
             span = period - move
@@ -288,6 +283,18 @@
                 low = jnp.where(place < span, k * low, 0.0)
                 out[0, :, block] += high - low
                 out[1 + d, :, block] -= high + low
+        for copy in copies[0:2]:
+            copy.wait_recv()
+        other = jnp.concatenate([chars[0, 0, 0, 16:32, :], ax[turn, 0]], axis=0)
+        jump = pltpu.roll(other, 64, 1) - chars[0, 0, 3]
+        jump = jnp.where(lane32 >= 64, k * jump, 0.0)
+        out[0, :, 384:512] += jump
+        out[1, :, 384:512] -= jump
+        other = jnp.concatenate([ax[turn, 1], chars[1, 0, 3, 0:16, :]], axis=0)
+        jump = chars[1, 0, 0] - pltpu.roll(other, 64, 1)
+        jump = jnp.where(lane32 < 64, k * jump, 0.0)
+        out[0, :, 0:128] -= jump
+        out[1, :, 0:128] -= jump
 
     loads[3].wait()
     for i in range(32):
@@ -324,15 +331,10 @@
         for c in range(5):
             target[c, 240:256, :] = carry[c]
 
-    def boundary(turn, target, gain, copies):
+    def boundary_yz(turn, target, gain, copies):
         half, visc = 0.5 * gain, viscosity * gain
         for copy in copies:
             copy.wait_recv()
-        lower, upper = [hx[turn, 0, c] for c in range(5)], [hx[turn, 1, c] for c in range(5)]
-        low_flux, up_flux = fluxes(lower)[0], fluxes(upper)[0]
-        for c in range(5):
-            target[c, 0:16, :] += visc * lower[c] + half * low_flux[c]
-            target[c, 240:256, :] += visc * upper[c] - half * up_flux[c]
         lower, upper = [hy[turn, 0, c] for c in range(5)], [hy[turn, 1, c] for c in range(5)]
         low_flux, up_flux = fluxes(lower)[1], fluxes(upper)[1]
         for c in range(5):
@@ -347,6 +349,22 @@
             visc * both[c] + jnp.where(odd, half * flux[c], -half * flux[c]) for c in range(5)
         ]
 
+    def boundary_x(turn, target, gain, copies):
+        half, visc = 0.5 * gain, viscosity * gain
+        outer = []
+        for side, rows, copy in ((0, slice(0, 16), copies[0]), (1, slice(240, 256), copies[1])):
+            copy.wait_recv()
+            state = [hx[turn, side, c] for c in range(5)]
+            flux = fluxes(state)[0]
+            values = []
+            for c in range(5):
+                term = half * flux[c] if side == 0 else -half * flux[c]
+                value = target[c, rows, :] + (visc * state[c] + term)
+                target[c, rows, :] = value
+                values.append(value)
+            outer.append(values)
+        return outer
+
     def add_edges(target, terms, x):
         values = []
         for c in range(5):
@@ -357,35 +375,42 @@
         return values
 
     interior(s0, s1, flow_step, lambda c, x, u: u)
-    terms = boundary(0, s1, flow_step, round_0)
-    pack_first_slab = [s1[c, 0:16, :] for c in range(5)]
-
-    def finish_first(x, packed):
-        return pack_lanes(packed, add_edges(s1, terms, x), x)
-
-    packed = lax.fori_loop(0, 16, finish_first, pack_first_slab)
+    terms = boundary_yz(0, s1, flow_step, round_yz)
+    packed = [s1[c, 16:32, :] for c in range(5)]
+    packed = lax.fori_loop(1, 15, lambda x, p: pack_lanes(p, add_edges(s1, terms, x), x), packed)
+    for x in (0, 15):
+        add_edges(s1, terms, x)
+    outer = boundary_x(0, s1, flow_step, round_x)
+    round_x = sends_x(1, lambda r: s1.at[:, r : r + 16, :], every)
+    packed = pack_lanes(pack_lanes(packed, outer[0], 0), outer[1], 15)
     for c in range(5):
         sz[1, c] = packed[c]
     pack_rows(1, s1, range(5))
-    round_1 = flow_sends(1, lambda r: s1.at[:, r : r + 16, :], every)
+    round_yz = sends_yz(1, every)
 
     interior(s1, s2, 0.5 * flow_step, lambda c, x, u: 0.5 * (s0[c, slab(x), :] + u))
-    terms_2 = boundary(1, s2, 0.5 * flow_step, round_1)
-
-    def finish_second(x, packed):
-        values = add_edges(s2, terms_2, x)
+    terms_2 = boundary_yz(1, s2, 0.5 * flow_step, round_yz)
+
+    def velocity(x, values):
         inverse = 1.0 / values[0]
         vx, vy, vz = (values[d] * inverse for d in (1, 2, 3))
         vel[0, slab(x), :], vel[1, slab(x), :], vel[2, slab(x), :] = vy, vz, vx
-        return pack_lanes(packed, [vy, vx], x)
+        return [vy, vx]
 
     zero = jnp.zeros((16, 128), F32)
-    packed = lax.fori_loop(0, 16, finish_second, [zero, zero])
-    sz[2, 0], sz[2, 1] = packed
+    packed = lax.fori_loop(
+        1, 15, lambda x, p: pack_lanes(p, velocity(x, add_edges(s2, terms_2, x)), x), [zero, zero]
+    )
+    for x in (0, 15):
+        add_edges(s2, terms_2, x)
+    outer = boundary_x(1, s2, 0.5 * flow_step, round_x)
+    outer = [velocity(0, outer[0]), velocity(15, outer[1])]
+    round_x = sends_x(2, lambda r: vel.at[0:2, r : r + 16, :], pl.ds(0, 2))
+    sz[2, 0], sz[2, 1] = pack_lanes(pack_lanes(packed, outer[0], 0), outer[1], 15)
     for i, comp in enumerate((1, 2)):
         sy[2, 0, i] = vel[comp, pl.ds(15, 16, stride=16), :]
         sy[2, 1, i] = vel[comp, pl.ds(0, 16, stride=16), :]
-    round_2 = flow_sends(2, lambda r: vel.at[0:2, r : r + 16, :], pl.ds(0, 2))
+    round_yz = sends_yz(2, pl.ds(0, 2))
 
     stores = [
         pltpu.make_async_copy(s2.at[0], rho_out, out_sem.at[0]),
@@ -417,12 +442,8 @@
         return carry
 
     lax.fori_loop(0, 16, curl, 0)
-    for copy in round_2:
+    for copy in round_yz:
         copy.wait_recv()
-    vort[1, 0:16, :] += hx[2, 0, 1]
-    vort[2, 0:16, :] -= hx[2, 0, 0]
-    vort[1, 240:256, :] -= hx[2, 1, 1]
-    vort[2, 240:256, :] += hx[2, 1, 0]
     vort[0, pl.ds(0, 16, stride=16), :] -= hy[2, 0, 0]
     vort[2, pl.ds(0, 16, stride=16), :] += hy[2, 0, 1]
     vort[0, pl.ds(15, 16, stride=16), :] += hy[2, 1, 0]
@@ -447,7 +468,15 @@
             mref[d, slab(a), :] = 0.0625 * sums[d]
         return carry
 
-    lax.fori_loop(0, 8, lamb_pair, 0)
+    lax.fori_loop(1, 7, lamb_pair, 0)
+    round_x[0].wait_recv()
+    vort[1, 0:16, :] += hx[2, 0, 1]
+    vort[2, 0:16, :] -= hx[2, 0, 0]
+    lamb_pair(0, 0)
+    round_x[1].wait_recv()
+    vort[1, 240:256, :] -= hx[2, 1, 1]
+    vort[2, 240:256, :] += hx[2, 1, 0]
+    lamb_pair(7, 0)
     coarse = [
         mref[d, pl.ds(0, 64, stride=2), :] + mref[d, pl.ds(1, 64, stride=2), :] for d in range(3)
     ]
@@ -529,6 +558,19 @@
     stores[-1].start()
     for copy in pending:
         copy.wait_send()
+    for store in stores:
+        store.wait()
+
+
+def hand_over(*refs):
+    sources, targets, held, sem = refs[0:4], refs[4:8], refs[8:12], refs[12]
+    loads = [pltpu.make_async_copy(sources[i], held[i], sem.at[0, i]) for i in range(4)]
+    stores = [pltpu.make_async_copy(held[i], targets[i], sem.at[1, i]) for i in range(4)]
+    for load in loads:
+        load.start()
+    for load, store in zip(loads, stores):
+        load.wait()
+        store.start()
     for store in stores:
         store.wait()
 
@@ -586,6 +628,15 @@
             acoustic.reshape(32, 4, 512), tile_slot, tile_element,
             *[jnp.asarray(c) for c in consts],
         )
+        outs = pl.pallas_call(
+            hand_over,
+            out_shape=out_shape,
+            in_specs=[anywhere] * 4,
+            out_specs=[anywhere] * 4,
+            scratch_shapes=[vmem(o.shape, F32) for o in out_shape]
+            + [pltpu.SemaphoreType.DMA((2, 4))],
+            compiler_params=pltpu.CompilerParams(vmem_limit_bytes=60 * 2**20),
+        )(*outs)
         return (
             outs[0].reshape(16, 16, 128), outs[1].reshape(3, 16, 16, 128),
             outs[2].reshape(16, 16, 128), outs[3].reshape(4, 2, 4, 4, 512),

time: 55.6 us -> 50.4 us (0.906)
  local copies, waits for them, and re-layouts: 5.07 us -> 0 us
    unnamed x8 -> x0, local copies, waits for them, and re-layouts: 5.07 us -> none
    pallas_call x1, Pallas kernels: 49.4 us -> 47 us  [on_device(): pl.pallas_call(functools.partial(kernel, zh_count, x_count, gy_count, gz_...]
    pallas_call x0 -> x1, Pallas kernels: none -> 2.01 us  [on_device(): pl.pallas_call(hand_over, out_shape=out_shape, in_specs=[anywhere] * 4, o...]
where the time goes in v1:
time: 50.4 us; the launch traced here: 49.7 us
  Pallas kernels  49 us (97%)
  between operations  0.64 us (1%)
    pallas_call x1, Pallas kernels, on_device(): pl.pallas_call(functools.partial(kernel, zh_count, x_count, gy_count, gz_...  47 us
    pallas_call x1, Pallas kernels, on_device(): pl.pallas_call(hand_over, out_shape=out_shape, in_specs=[anywhere] * 4, o...  2.01 us

profile of v1, /device:TPU:2, one launch (start us, length us, event | category | flops | bytes accessed | tf_op | source)
XLA Modules:
  0.0 49.7 jit_solution(2624359277051908712)
XLA Ops:
  0.6 47.0 %shard_map.156 = (f32[256,128]{1,0:T(8,128)}, f32[3,256,128]{2,1,0:T(8,128)}, f32[256,128]{1,0:T(8,128)}, f32[32,4,512]{2,1,0:T(4,128)}) custom-call(f32[256,128]{1,0:T(8,128)} %bitcast.12, f32[3,256,128]{2,1,0:T(8,128)} %bitcast.8, f32[256,128]{1,0:T(8,128)} %bitcast.13, f32[32,4,512]{2,1,0:T(4,128)} %bitcast.10, s32[1,1,1,8]{3,2,1,0:T(1,128)} %slot_ref.1, ...), custom_call_target="tpu_custom_call" | custom-call | flops 1000000000 | bytes 4194304 | tf_op jit(solution)/shard_map/pallas_call | solution.py:614
  47.6 2.0 %shard_map.157 = (f32[256,128]{1,0:T(8,128)}, f32[3,256,128]{2,1,0:T(8,128)}, f32[256,128]{1,0:T(8,128)}, f32[32,4,512]{2,1,0:T(4,128)}) custom-call(f32[256,128]{1,0:T(8,128)} %get-tuple-element.12.refs_0_, f32[3,256,128]{2,1,0:T(8,128)} %get-tuple-element.13.refs_1_, f32[256,128]{1,0:T(8,128)} %get-tuple-element.14.refs_2_, ...), custom_call_target="tpu_custom_call" | custom-call | tf_op jit(solution)/shard_map/pallas_call | solution.py:631

commit v2 on v1

--- a/solution.py
+++ b/solution.py
@@ -101,7 +101,7 @@
     rho_hbm, mom_hbm, energy_hbm, sound_hbm, slot_ref, element_ref,
     dxh_hbm, dxl_hbm, dyh_hbm, dyl_hbm, dzh_hbm, dzl_hbm, order_hbm,
     rho_out, mom_out, energy_out, sound_out,
-    s0, s1, s2, vel, vort, mref, fref, tiles,
+    s0, s1, s2, vel, vort, mref, fref, tiles, parcel, arrived, full,
     hx, hy, hz, sy, sz, ax, ay, az, axs, ays, azs,
     stage, q0, q1, n0, chars, near,
     dxh, dxl, dyh, dyl, dzh, dzl, order,
@@ -504,49 +504,71 @@
     parts = jnp.dot(parts, order[...], preferred_element_type=F32)
     own = parts[0:24] + parts[24:48] + parts[48:72]
     for d in range(3):
-        tiles[gx, :, 512 * d : 512 * d + 512] = own[8 * d : 8 * d + 8]
-    row8 = iota((8, 128), 0)
-    target = jnp.zeros((8, 128), jnp.int32)
+        tiles[0, :, 512 * d : 512 * d + 512] = own[8 * d : 8 * d + 8]
+    row8, lane8 = iota((8, 128), 0), iota((8, 128), 1)
+    label = jnp.full((8, 128), -1, jnp.int32)
     for t in range(8):
-        address = lax.div(slot_ref[0, 0, 0, t], 4) * 32 + element_ref[0, 0, 0, t]
-        target = jnp.where(row8 == t, address, target)
-    tiles[gx, :, 1536:1664] = target.astype(F32)
-
-    def tile_copy(i, source, device):
-        return send(tiles.at[source], tiles.at[source], tile_send.at[i], tile_recv.at[i], device)
-
-    down = [tile_copy(k - 1, gx, at_zh(k)) for k in range(1, zh_count)]
+        label = jnp.where((lane8 < 24) & (lax.rem(lane8, 8) == t), slot_ref[0, 0, 0, t], label)
+        label = jnp.where((lane8 >= 64) & (row8 == t), element_ref[0, 0, 0, t], label)
+    tiles[0, :, 1536:1664] = label.astype(F32)
+
+    down = [
+        send(tiles.at[0], tiles.at[k], tile_send.at[k - 1], tile_recv.at[k - 1], at_zh(k))
+        for k in range(1, zh_count)
+    ]
     across = []
+    slots = 4 * x_count
+    place = iota((slots, 24), 0)
+    wanted = zh * slots + lax.rem(xi + place // 4, x_count) * 4 + lax.rem(place, 4)
+    wanted = wanted.astype(F32)
 
     def pass_on(k):
-        source = lax.rem(zh - k + zh_count, zh_count) * x_count + xi
+        listed = jnp.broadcast_to(tiles[k, 0:1, 1536:1560], (slots, 24))
+        choice = jnp.where(listed == wanted, 1.0, 0.0).astype(BF16)
+        for first in range(0, TILE_LANES, 512):
+            block = slice(first, min(first + 512, TILE_LANES))
+            high, rest = halves(tiles[k, :, block])
+            middle, low = halves(rest)
+            parts = jnp.concatenate([high, middle, low], axis=0).astype(BF16)
+            chosen = jnp.dot(choice, parts, preferred_element_type=F32)
+            full[k * slots : k * slots + 4, block] = chosen[0:4]
+            for j in range(1, x_count):
+                parcel[k, j - 1, :, block] = chosen[4 * j : 4 * j + 4]
         for j in range(1, x_count):
             i = zh_count - 1 + k * (x_count - 1) + j - 1
-            across.append(tile_copy(i, source, at_xi(j)))
+            across.append(
+                send(
+                    parcel.at[k, j - 1], arrived.at[k, j - 1], tile_send.at[i], tile_recv.at[i],
+                    at_xi(j),
+                )
+            )
 
     pass_on(0)
 
     for load in loads[5:]:
         load.wait()
     rates(q0, q1, sound_step, lambda c: q0[c], faces_0, 0, True)
-    for k in range(1, zh_count):
+    faces_1 = face_sends(1, q1)
+    for k in sorted(range(1, zh_count), key=lambda k: min(k, zh_count - k)):
         down[k - 1].wait_recv()
         pass_on(k)
-    faces_1 = face_sends(1, q1)
     rates(q1, n0, 0.5 * sound_step, lambda c: 0.5 * (q0[c] + q1[c]), faces_1, 1, True)
 
-    for copy in across:
+    for i, copy in enumerate(across):
         copy.wait_recv()
-    gx_tiles = 8 * gx_count
-    address = tiles[:, :, 1536:1664].reshape(gx_tiles, 128)
-    wanted = (gx * 32 + iota((gx_tiles, 128), 1)).astype(F32)
-    picking = jnp.where(address == wanted, 1.0, 0.0)
-    picking = jnp.transpose(picking)[0:32].astype(BF16)
+    for k in range(zh_count):
+        for j in range(1, x_count):
+            top = k * slots + 4 * j
+            full[top : top + 4, :] = arrived[k, j - 1]
+    count = zh_count * slots
+    element = (iota((count, 128), 1) - 64).astype(F32)
+    picking = jnp.where(full[:, 1536:1664] == element, 1.0, 0.0)
+    picking = jnp.concatenate([picking, picking], axis=0)
+    picking = jnp.transpose(picking)[64:96].astype(BF16)
     for d in range(3):
-        block = tiles[:, :, 512 * d : 512 * d + 512].reshape(gx_tiles, 512)
-        high, low = halves(block)
-        both = jnp.dot(picking, high.astype(BF16), preferred_element_type=F32)
-        both += jnp.dot(picking, low.astype(BF16), preferred_element_type=F32)
+        high, low = halves(full[:, 512 * d : 512 * d + 512])
+        parts = jnp.concatenate([high, low], axis=0).astype(BF16)
+        both = jnp.dot(picking, parts, preferred_element_type=F32)
         q1[1 + d] = -source_gain * sound_step * both
     q1[0] = jnp.zeros((32, 512), F32)
     faces_2 = face_sends(2, q1)
@@ -595,7 +617,10 @@
         scratch = [
             vmem((5, 256, 128), F32), vmem((5, 256, 128), F32), vmem((5, 256, 128), F32),
             vmem((3, 256, 128), F32), vmem((3, 256, 128), F32), vmem((3, 128, 128), F32),
-            vmem((2, 128, 128), F32), vmem((gx_count, 8, TILE_LANES), F32),
+            vmem((2, 128, 128), F32), vmem((zh_count, 8, TILE_LANES), F32),
+            vmem((zh_count, x_count - 1, 4, TILE_LANES), F32),
+            vmem((zh_count, x_count - 1, 4, TILE_LANES), F32),
+            vmem((4 * gx_count, TILE_LANES), F32),
             vmem((3, 2, 5, 16, 128), F32), vmem((3, 2, 5, 16, 128), F32),
             vmem((3, 2, 5, 16, 128), F32), vmem((3, 2, 5, 16, 128), F32),
             vmem((3, 5, 16, 128), F32),

time: 50.4 us -> 47.3 us (0.938)
  Pallas kernels: 49 us -> 45.9 us
    pallas_call x1, Pallas kernels: 47 us -> 43.9 us  [on_device(): pl.pallas_call(functools.partial(kernel, zh_count, x_count, gy_count, gz_...]
where the time goes in v2:
time: 47.3 us; the launch traced here: 46.6 us
  Pallas kernels  45.9 us (97%)
  between operations  0.64 us (1%)
    pallas_call x1, Pallas kernels, on_device(): pl.pallas_call(functools.partial(kernel, zh_count, x_count, gy_count, gz_...  43.9 us
    pallas_call x1, Pallas kernels, on_device(): pl.pallas_call(hand_over, out_shape=out_shape, in_specs=[anywhere] * 4, o...  2.01 us

profile of v2, /device:TPU:2, one launch (start us, length us, event | category | flops | bytes accessed | tf_op | source)
XLA Modules:
  0.0 46.6 jit_solution(17580980652311668664)
XLA Ops:
  0.6 43.9 %shard_map.156 = (f32[256,128]{1,0:T(8,128)}, f32[3,256,128]{2,1,0:T(8,128)}, f32[256,128]{1,0:T(8,128)}, f32[32,4,512]{2,1,0:T(4,128)}) custom-call(f32[256,128]{1,0:T(8,128)} %bitcast.12, f32[3,256,128]{2,1,0:T(8,128)} %bitcast.8, f32[256,128]{1,0:T(8,128)} %bitcast.13, f32[32,4,512]{2,1,0:T(4,128)} %bitcast.10, s32[1,1,1,8]{3,2,1,0:T(1,128)} %slot_ref.1, ...), custom_call_target="tpu_custom_call" | custom-call | flops 1000000000 | bytes 4194304 | tf_op jit(solution)/shard_map/pallas_call | solution.py:639
  44.6 2.0 %shard_map.157 = (f32[256,128]{1,0:T(8,128)}, f32[3,256,128]{2,1,0:T(8,128)}, f32[256,128]{1,0:T(8,128)}, f32[32,4,512]{2,1,0:T(4,128)}) custom-call(f32[256,128]{1,0:T(8,128)} %get-tuple-element.12.refs_0_, f32[3,256,128]{2,1,0:T(8,128)} %get-tuple-element.13.refs_1_, f32[256,128]{1,0:T(8,128)} %get-tuple-element.14.refs_2_, ...), custom_call_target="tpu_custom_call" | custom-call | tf_op jit(solution)/shard_map/pallas_call | solution.py:656

commit v3 on v2

--- a/solution.py
+++ b/solution.py
@@ -19,6 +19,7 @@
 lift_factor = 28.0
 source_gain = 40.0
 TILE_LANES = 1664
+PARCEL_LANES = 1920
 
 
 def derivative_numbers():
@@ -220,9 +221,11 @@
         def go(i, src, dst, device):
             return send(src, dst, face_send.at[turn, i], face_recv.at[turn, i], device)
 
-        return [
+        along_x = [
             go(0, axs.at[turn, 0], ax.at[turn, 0], at_x(-1)),
             go(1, axs.at[turn, 1], ax.at[turn, 1], at_x(1)),
+        ]
+        return along_x + [
             go(2, ays.at[turn, 0], ay.at[turn, 0], at_y(-1)),
             go(3, ays.at[turn, 1], ay.at[turn, 1], at_y(1)),
             go(4, azs.at[turn, 0], az.at[turn, 0], at_z(-1)),
@@ -284,7 +287,8 @@
                 out[0, :, block] += high - low
                 out[1 + d, :, block] -= high + low
         for copy in copies[0:2]:
-            copy.wait_recv()
+            if copy is not None:
+                copy.wait_recv()
         other = jnp.concatenate([chars[0, 0, 0, 16:32, :], ax[turn, 0]], axis=0)
         jump = pltpu.roll(other, 64, 1) - chars[0, 0, 3]
         jump = jnp.where(lane32 >= 64, k * jump, 0.0)
@@ -389,6 +393,10 @@
     round_yz = sends_yz(1, every)
 
     interior(s1, s2, 0.5 * flow_step, lambda c, x, u: 0.5 * (s0[c, slab(x), :] + u))
+    for load in loads[5:]:
+        load.wait()
+    rates(q0, q1, sound_step, lambda c: q0[c], faces_0, 0, True)
+    faces_1 = face_sends(1, q1)
     terms_2 = boundary_yz(1, s2, 0.5 * flow_step, round_yz)
 
     def velocity(x, values):
@@ -442,6 +450,7 @@
         return carry
 
     lax.fori_loop(0, 16, curl, 0)
+    rates(q1, n0, 0.5 * sound_step, lambda c: 0.5 * (q0[c] + q1[c]), faces_1, 1, True)
     for copy in round_yz:
         copy.wait_recv()
     vort[0, pl.ds(0, 16, stride=16), :] -= hy[2, 0, 0]
@@ -506,34 +515,50 @@
     for d in range(3):
         tiles[0, :, 512 * d : 512 * d + 512] = own[8 * d : 8 * d + 8]
     row8, lane8 = iota((8, 128), 0), iota((8, 128), 1)
-    label = jnp.full((8, 128), -1, jnp.int32)
+    label = jnp.zeros((8, 128), jnp.int32)
     for t in range(8):
-        label = jnp.where((lane8 < 24) & (lax.rem(lane8, 8) == t), slot_ref[0, 0, 0, t], label)
-        label = jnp.where((lane8 >= 64) & (row8 == t), element_ref[0, 0, 0, t], label)
+        both = jnp.where(lane8 < 64, slot_ref[0, 0, 0, t], element_ref[0, 0, 0, t])
+        label = jnp.where(row8 == t, both, label)
     tiles[0, :, 1536:1664] = label.astype(F32)
 
     down = [
-        send(tiles.at[0], tiles.at[k], tile_send.at[k - 1], tile_recv.at[k - 1], at_zh(k))
-        for k in range(1, zh_count)
+        (k, send(tiles.at[0], tiles.at[k], tile_send.at[k - 1], tile_recv.at[k - 1], at_zh(k)))
+        for k in sorted(range(1, zh_count), key=lambda k: -min(k, zh_count - k))
     ]
+    down.sort(key=lambda item: item[0])
     across = []
     slots = 4 * x_count
-    place = iota((slots, 24), 0)
-    wanted = zh * slots + lax.rem(xi + place // 4, x_count) * 4 + lax.rem(place, 4)
-    wanted = wanted.astype(F32)
+    place = iota((slots, 128), 0)
+    peer = zh * x_count + lax.rem(xi + place // 4, x_count)
+
+    def slot_of(step):
+        owner = lax.rem(peer + step + gx_count, gx_count)
+        return (owner * 4 + lax.rem(place, 4)).astype(F32)
+
+    wanted, wanted_after, wanted_before = slot_of(0), slot_of(1), slot_of(-1)
 
     def pass_on(k):
-        listed = jnp.broadcast_to(tiles[k, 0:1, 1536:1560], (slots, 24))
-        choice = jnp.where(listed == wanted, 1.0, 0.0).astype(BF16)
-        for first in range(0, TILE_LANES, 512):
-            block = slice(first, min(first + 512, TILE_LANES))
-            high, rest = halves(tiles[k, :, block])
-            middle, low = halves(rest)
-            parts = jnp.concatenate([high, middle, low], axis=0).astype(BF16)
-            chosen = jnp.dot(choice, parts, preferred_element_type=F32)
+        marks = tiles[k, :, 1536:1664]
+        named = jnp.where(lane8 < 64, marks, pltpu.roll(marks, 64, 1))
+        named = [jnp.broadcast_to(named[t : t + 1], (slots, 128)) for t in range(8)]
+
+        def pick(hits, value, block):
+            chosen = jnp.zeros((slots, 128), F32)
+            for t in range(8):
+                row = jnp.broadcast_to(value[t : t + 1], (slots, 128))
+                chosen = jnp.where(hits[t], row, chosen)
             full[k * slots : k * slots + 4, block] = chosen[0:4]
             for j in range(1, x_count):
                 parcel[k, j - 1, :, block] = chosen[4 * j : 4 * j + 4]
+
+        hits = [n == wanted for n in named]
+        for first in range(0, TILE_LANES, 128):
+            block = slice(first, first + 128)
+            pick(hits, tiles[k, :, block], block)
+        low_face = jnp.where(lane8 < 64, tiles[k, :, 0:128], marks)
+        pick([n == wanted_after for n in named], low_face, slice(1664, 1792))
+        high_face = jnp.where(lane8 < 64, pltpu.roll(marks, 64, 1), tiles[k, :, 384:512])
+        pick([n == wanted_before for n in named], high_face, slice(1792, 1920))
         for j in range(1, x_count):
             i = zh_count - 1 + k * (x_count - 1) + j - 1
             across.append(
@@ -545,15 +570,9 @@
 
     pass_on(0)
 
-    for load in loads[5:]:
-        load.wait()
-    rates(q0, q1, sound_step, lambda c: q0[c], faces_0, 0, True)
-    faces_1 = face_sends(1, q1)
     for k in sorted(range(1, zh_count), key=lambda k: min(k, zh_count - k)):
-        down[k - 1].wait_recv()
+        down[k - 1][1].wait_recv()
         pass_on(k)
-    rates(q1, n0, 0.5 * sound_step, lambda c: 0.5 * (q0[c] + q1[c]), faces_1, 1, True)
-
     for i, copy in enumerate(across):
         copy.wait_recv()
     for k in range(zh_count):
@@ -561,18 +580,63 @@
             top = k * slots + 4 * j
             full[top : top + 4, :] = arrived[k, j - 1]
     count = zh_count * slots
-    element = (iota((count, 128), 1) - 64).astype(F32)
+    lanes = iota((count, 128), 1)
+    element = (lanes - 64).astype(F32)
     picking = jnp.where(full[:, 1536:1664] == element, 1.0, 0.0)
     picking = jnp.concatenate([picking, picking], axis=0)
     picking = jnp.transpose(picking)[64:96].astype(BF16)
-    for d in range(3):
+
+    def pick_source(d):
         high, low = halves(full[:, 512 * d : 512 * d + 512])
         parts = jnp.concatenate([high, low], axis=0).astype(BF16)
         both = jnp.dot(picking, parts, preferred_element_type=F32)
         q1[1 + d] = -source_gain * sound_step * both
-    q1[0] = jnp.zeros((32, 512), F32)
-    faces_2 = face_sends(2, q1)
-    rates(q1, q0, 0.5 * sound_step, lambda c: n0[c] + q1[c], faces_2, 2, False)
+
+    pick_source(1)
+    pick_source(2)
+    faces_2 = []
+    for d, (kept, landing, device) in enumerate(((ays, ay, at_y), (azs, az, at_z))):
+        for side in (0, 1):
+            for j in range(4):
+                block = slice(128 * j, 128 * j + 128)
+                value = q1[2 + d, :, block] if side else -q1[2 + d, :, block]
+                chars[side, 1 + d, j] = value
+                if d == 0:
+                    top = 12 * side
+                    kept[2, side, 0:4, block] = chars[side, 1, j, top : top + 4, :]
+                    kept[2, side, 4:8, block] = chars[side, 1, j, top + 16 : top + 20, :]
+                else:
+                    kept[2, side, :, block] = chars[side, 2, j, pl.ds(3 * side, 8, stride=4), :]
+            i = 2 + 2 * d + side
+            faces_2.append(
+                send(
+                    kept.at[2, side], landing.at[2, side], face_send.at[2, i],
+                    face_recv.at[2, i], device(2 * side - 1),
+                )
+            )
+    pick_source(0)
+    for j in range(4):
+        block = slice(128 * j, 128 * j + 128)
+        chars[0, 0, j] = -q1[1, :, block]
+        chars[1, 0, j] = q1[1, :, block]
+    after, before = full[:, 1664:1792], full[:, 1792:1920]
+    picking_2 = jnp.concatenate(
+        [
+            jnp.where((lanes >= 64) & (after == element), 1.0, 0.0),
+            jnp.where((lanes < 64) & (before == element + 80.0), 1.0, 0.0),
+        ],
+        axis=0,
+    )
+    if 2 * count < 128:
+        picking_2 = jnp.concatenate([picking_2, jnp.zeros((128 - 2 * count, 128), F32)], axis=0)
+    picking_2 = jnp.transpose(picking_2)[:, 0 : 2 * count]
+    picking_2 = jnp.concatenate([picking_2[64:80], picking_2[0:16]], axis=0).astype(BF16)
+    high, low = halves(jnp.concatenate([after, before], axis=0))
+    sides = jnp.dot(picking_2, high.astype(BF16), preferred_element_type=F32)
+    sides += jnp.dot(picking_2, low.astype(BF16), preferred_element_type=F32)
+    ax[2, 0] = source_gain * sound_step * sides[0:16]
+    ax[2, 1] = -source_gain * sound_step * sides[16:32]
+    rates(q1, q0, 0.5 * sound_step, lambda c: n0[c] + (q1[c] if c else 0.0), [None, None] + faces_2, 2, False)
     for i in range(32):
         c, part = i // 8, i % 8
         stage[i] = q0[c, 4 * part : 4 * part + 4, :]
@@ -585,16 +649,11 @@
 
 
 def hand_over(*refs):
-    sources, targets, held, sem = refs[0:4], refs[4:8], refs[8:12], refs[12]
-    loads = [pltpu.make_async_copy(sources[i], held[i], sem.at[0, i]) for i in range(4)]
-    stores = [pltpu.make_async_copy(held[i], targets[i], sem.at[1, i]) for i in range(4)]
-    for load in loads:
-        load.start()
-    for load, store in zip(loads, stores):
-        load.wait()
-        store.start()
-    for store in stores:
-        store.wait()
+    copies = [pltpu.make_async_copy(refs[i], refs[4 + i], refs[8].at[i]) for i in range(4)]
+    for copy in copies:
+        copy.start()
+    for copy in copies:
+        copy.wait()
 
 
 def solution(mesh):
@@ -606,6 +665,7 @@
 
     def on_device(density, momentum, energy, acoustic, tile_slot, tile_element):
         anywhere = pl.BlockSpec(memory_space=pl.ANY)
+        in_hbm = pl.BlockSpec(memory_space=pltpu.HBM)
         scalars = pl.BlockSpec(memory_space=pltpu.SMEM)
         out_shape = (
             jax.ShapeDtypeStruct((256, 128), F32),
@@ -618,14 +678,14 @@
             vmem((5, 256, 128), F32), vmem((5, 256, 128), F32), vmem((5, 256, 128), F32),
             vmem((3, 256, 128), F32), vmem((3, 256, 128), F32), vmem((3, 128, 128), F32),
             vmem((2, 128, 128), F32), vmem((zh_count, 8, TILE_LANES), F32),
-            vmem((zh_count, x_count - 1, 4, TILE_LANES), F32),
-            vmem((zh_count, x_count - 1, 4, TILE_LANES), F32),
-            vmem((4 * gx_count, TILE_LANES), F32),
+            vmem((zh_count, x_count - 1, 4, PARCEL_LANES), F32),
+            vmem((zh_count, x_count - 1, 4, PARCEL_LANES), F32),
+            vmem((4 * gx_count, PARCEL_LANES), F32),
             vmem((3, 2, 5, 16, 128), F32), vmem((3, 2, 5, 16, 128), F32),
             vmem((3, 2, 5, 16, 128), F32), vmem((3, 2, 5, 16, 128), F32),
             vmem((3, 5, 16, 128), F32),
             vmem((3, 2, 16, 128), F32), vmem((3, 2, 8, 512), F32), vmem((3, 2, 8, 512), F32),
-            vmem((3, 2, 16, 128), F32), vmem((3, 2, 8, 512), F32), vmem((3, 2, 8, 512), F32),
+            vmem((2, 2, 16, 128), F32), vmem((3, 2, 8, 512), F32), vmem((3, 2, 8, 512), F32),
             vmem((32, 4, 512), F32), vmem((4, 32, 512), F32), vmem((4, 32, 512), F32),
             vmem((4, 32, 512), F32), vmem((2, 3, 4, 32, 128), F32), vmem((2, 2, 4, 32, 128), F32),
             vmem((512, 512), BF16), vmem((512, 512), BF16), vmem((256, 256), BF16),
@@ -636,14 +696,15 @@
             pltpu.SemaphoreType.DMA((3, 6)), pltpu.SemaphoreType.DMA((3, 6)),
             pltpu.SemaphoreType.DMA((tile_sends,)), pltpu.SemaphoreType.DMA((tile_sends,)),
         ]
+        held_shape = tuple(pltpu.VMEM(o.shape, F32) for o in out_shape)
         outs = pl.pallas_call(
             functools.partial(kernel, zh_count, x_count, gy_count, gz_count),
-            out_shape=out_shape,
+            out_shape=held_shape,
             in_specs=[anywhere] * 4 + [scalars] * 2 + [anywhere] * 7,
             out_specs=[anywhere] * 4,
             scratch_shapes=scratch,
             compiler_params=pltpu.CompilerParams(
-                collective_id=0, has_side_effects=True, vmem_limit_bytes=60 * 2**20
+                collective_id=0, has_side_effects=True, vmem_limit_bytes=57 * 2**20
             ),
             cost_estimate=pl.CostEstimate(
                 flops=10**9, bytes_accessed=4 * 2**20, transcendentals=0
@@ -657,10 +718,9 @@
             hand_over,
             out_shape=out_shape,
             in_specs=[anywhere] * 4,
-            out_specs=[anywhere] * 4,
-            scratch_shapes=[vmem(o.shape, F32) for o in out_shape]
-            + [pltpu.SemaphoreType.DMA((2, 4))],
-            compiler_params=pltpu.CompilerParams(vmem_limit_bytes=60 * 2**20),
+            out_specs=[in_hbm] * 4,
+            scratch_shapes=[pltpu.SemaphoreType.DMA((4,))],
+            compiler_params=pltpu.CompilerParams(vmem_limit_bytes=8 * 2**20),
         )(*outs)
         return (
             outs[0].reshape(16, 16, 128), outs[1].reshape(3, 16, 16, 128),

time: 47.3 us -> 45.5 us (0.962); the launches traced: 46.6 us -> 45.4 us
  Pallas kernels: 45.9 us -> 44.7 us
    pallas_call x1, Pallas kernels: 2.01 us -> 0.96 us  [on_device(): pl.pallas_call(hand_over, out_shape=out_shape, in_specs=[anywhere] * 4, o...]
where the time goes in v3:
time: 45.5 us; the launch traced here: 45.4 us
  Pallas kernels  44.7 us (98%)
  between operations  0.64 us (1%)
    pallas_call x1, Pallas kernels, on_device(): pl.pallas_call(functools.partial(kernel, zh_count, x_count, gy_count, gz_...  43.8 us
    pallas_call x1, Pallas kernels, on_device(): pl.pallas_call(hand_over, out_shape=out_shape, in_specs=[anywhere] * 4, o...  0.96 us

profile of v3, /device:TPU:2, one launch (start us, length us, event | category | flops | bytes accessed | tf_op | source)
XLA Modules:
  0.0 45.4 jit_solution(15142323228153283558)
XLA Ops:
  0.6 43.8 %shard_map.156 = (f32[256,128]{1,0:T(8,128)S(1)}, f32[3,256,128]{2,1,0:T(8,128)S(1)}, f32[256,128]{1,0:T(8,128)S(1)}, f32[32,4,512]{2,1,0:T(4,128)S(1)}) custom-call(f32[256,128]{1,0:T(8,128)} %bitcast.12, f32[3,256,128]{2,1,0:T(8,128)} %bitcast.8, f32[256,128]{1,0:T(8,128)} %bitcast.13, f32[32,4,512]{2,1,0:T(4,128)} %bitcast.10, s32[1,1,1,8]{3,2,1,0:T(1,128)} %slot_ref.1, ...), custom_call_target="tpu_custom_call" | custom-call | flops 1000000000 | bytes 4194304 | tf_op jit(solution)/shard_map/pallas_call | solution.py:700
  44.4 1.0 %shard_map.157 = (f32[256,128]{1,0:T(8,128)}, f32[3,256,128]{2,1,0:T(8,128)}, f32[256,128]{1,0:T(8,128)}, f32[32,4,512]{2,1,0:T(4,128)}) custom-call(f32[256,128]{1,0:T(8,128)S(1)} %get-tuple-element.12.refs_0_, f32[3,256,128]{2,1,0:T(8,128)S(1)} %get-tuple-element.13.refs_1_, f32[256,128]{1,0:T(8,128)S(1)} %get-tuple-element.14.refs_2_, ...), custom_call_target="tpu_custom_call" | custom-call | tf_op jit(solution)/shard_map/pallas_call | solution.py:717

commit v4 on v3

--- a/solution.py
+++ b/solution.py
@@ -18,8 +18,9 @@
 sound_step = 0.02
 lift_factor = 28.0
 source_gain = 40.0
-TILE_LANES = 1664
-PARCEL_LANES = 1920
+TILE_LANES = 1536
+PARCEL_LANES = 1664
+PARTS = 2
 
 
 def derivative_numbers():
@@ -102,14 +103,16 @@
     rho_hbm, mom_hbm, energy_hbm, sound_hbm, slot_ref, element_ref,
     dxh_hbm, dxl_hbm, dyh_hbm, dyl_hbm, dzh_hbm, dzl_hbm, order_hbm,
     rho_out, mom_out, energy_out, sound_out,
-    s0, s1, s2, vel, vort, mref, fref, tiles, parcel, arrived, full,
+    s0, s1, s2, vel, vort, mref, fref, tiles, parcel, arrived, full, labels, named_elements,
     hx, hy, hz, sy, sz, ax, ay, az, axs, ays, azs,
     stage, q0, q1, n0, chars, near,
     dxh, dxl, dyh, dyl, dzh, dzl, order,
     in_sem, out_sem, flow_send, flow_recv, face_send, face_recv, tile_send, tile_recv,
+    label_send, label_recv,
 ):
     gx, gy, gz = lax.axis_index("gx"), lax.axis_index("gy"), lax.axis_index("gz")
     gx_count = zh_count * x_count
+    tile_sends = (zh_count - 1) + zh_count * (x_count - 1)
     zh, xi = gx // x_count, lax.rem(gx, x_count)
 
     def at_x(step):
@@ -202,6 +205,17 @@
     every = pl.ds(0, 5)
     round_x = sends_x(0, lambda r: s0.at[:, r : r + 16, :], every)
     round_yz = sends_yz(0, every)
+
+    row8, lane8 = iota((8, 128), 0), iota((8, 128), 1)
+    label = jnp.zeros((8, 128), jnp.int32)
+    for t in range(8):
+        both = jnp.where(lane8 < 64, slot_ref[0, 0, 0, t], element_ref[0, 0, 0, t])
+        label = jnp.where(row8 == t, both, label)
+    labels[0, 0] = label.astype(F32)
+    labels_down = [
+        send(labels.at[0, 0], labels.at[0, k], label_send.at[k - 1], label_recv.at[k - 1], at_zh(k))
+        for k in range(1, zh_count)
+    ]
 
     def face_sends(turn, q):
         for d in range(3):
@@ -263,6 +277,22 @@
                 out[1 + d] = base(1 + d)
             total = both if total is None else total + both
         out[0] = base(0) - gain * total
+        k = 0.5 * lift_factor * gain
+
+        def lift_x():
+            other = jnp.concatenate([chars[0, 0, 0, 16:32, :], ax[turn, 0]], axis=0)
+            jump = pltpu.roll(other, 64, 1) - chars[0, 0, 3]
+            jump = jnp.where(lane32 >= 64, k * jump, 0.0)
+            out[0, :, 384:512] += jump
+            out[1, :, 384:512] -= jump
+            other = jnp.concatenate([ax[turn, 1], chars[1, 0, 3, 0:16, :]], axis=0)
+            jump = chars[1, 0, 0] - pltpu.roll(other, 64, 1)
+            jump = jnp.where(lane32 < 64, k * jump, 0.0)
+            out[0, :, 0:128] -= jump
+            out[1, :, 0:128] -= jump
+
+        if not copies[0]:
+            lift_x()
         for side, d, move in ((0, 1, 28), (1, 1, 4), (0, 2, 31), (1, 2, 1)):
             for j in range(4):
                 near[side, d - 1, j] = pltpu.roll(chars[side, d, j], move, 0)
@@ -274,7 +304,6 @@
                 near[side, 0, j, top : top + 4, :] = ay[turn, side, 0:4, block]
                 near[side, 0, j, top + 16 : top + 20, :] = ay[turn, side, 4:8, block]
                 near[side, 1, j, pl.ds(3 - 3 * side, 8, stride=4), :] = az[turn, side, :, block]
-        k = 0.5 * lift_factor * gain
         for d, period, move in ((1, 64, 56), (2, 8, 7)):
             place = lax.rem(lane32, period)
             span = period - move
@@ -286,19 +315,10 @@
                 low = jnp.where(place < span, k * low, 0.0)
                 out[0, :, block] += high - low
                 out[1 + d, :, block] -= high + low
-        for copy in copies[0:2]:
-            if copy is not None:
+        if copies[0]:
+            for copy in copies[0:2]:
                 copy.wait_recv()
-        other = jnp.concatenate([chars[0, 0, 0, 16:32, :], ax[turn, 0]], axis=0)
-        jump = pltpu.roll(other, 64, 1) - chars[0, 0, 3]
-        jump = jnp.where(lane32 >= 64, k * jump, 0.0)
-        out[0, :, 384:512] += jump
-        out[1, :, 384:512] -= jump
-        other = jnp.concatenate([ax[turn, 1], chars[1, 0, 3, 0:16, :]], axis=0)
-        jump = chars[1, 0, 0] - pltpu.roll(other, 64, 1)
-        jump = jnp.where(lane32 < 64, k * jump, 0.0)
-        out[0, :, 0:128] -= jump
-        out[1, :, 0:128] -= jump
+            lift_x()
 
     loads[3].wait()
     for i in range(32):
@@ -397,6 +417,12 @@
         load.wait()
     rates(q0, q1, sound_step, lambda c: q0[c], faces_0, 0, True)
     faces_1 = face_sends(1, q1)
+    for copy in labels_down:
+        copy.wait_recv()
+    labels_across = [
+        send(labels.at[0], labels.at[j], label_send.at[i], label_recv.at[i], at_xi(j))
+        for j, i in zip(range(1, x_count), range(zh_count - 1, zh_count + x_count - 2))
+    ]
     terms_2 = boundary_yz(1, s2, 0.5 * flow_step, round_yz)
 
     def velocity(x, values):
@@ -451,6 +477,38 @@
 
     lax.fori_loop(0, 16, curl, 0)
     rates(q1, n0, 0.5 * sound_step, lambda c: 0.5 * (q0[c] + q1[c]), faces_1, 1, True)
+
+    slots = 4 * x_count
+    count = zh_count * slots
+    for copy in labels_across:
+        copy.wait_recv()
+    for step, owner in enumerate((gx, lax.rem(gx + 1, gx_count), lax.rem(gx - 1 + gx_count, gx_count))):
+        mine = (owner * 4 + lax.rem(row8, 4)).astype(F32)
+        for k in range(zh_count):
+            for j in range(x_count):
+                mark = labels[j, k]
+                turned = pltpu.roll(mark, 64, 1)
+                slot_names = jnp.where(lane8 < 64, mark, turned)
+                elements = jnp.where(lane8 < 64, turned, mark)
+                found = jnp.full((8, 128), -1.0, F32)
+                for t in range(8):
+                    hit = jnp.broadcast_to(slot_names[t : t + 1], (8, 128)) == mine
+                    element = jnp.broadcast_to(elements[t : t + 1], (8, 128))
+                    found = jnp.where(hit, element, found)
+                top = k * slots + 4 * j
+                named_elements[step, top : top + 4, :] = found[0:4]
+    lanes = iota((count, 128), 1)
+    element = lanes.astype(F32)
+    picking = jnp.where(named_elements[0] == element, 1.0, 0.0)
+    picking = jnp.transpose(jnp.concatenate([picking, picking], axis=0))[0:32].astype(BF16)
+    picking_2 = jnp.concatenate(
+        [
+            jnp.where((lanes < 16) & (named_elements[1] == element), 1.0, 0.0),
+            jnp.where((lanes >= 16) & (named_elements[2] == element), 1.0, 0.0),
+        ],
+        axis=0,
+    )
+    picking_2 = jnp.transpose(picking_2)[0:32].astype(BF16)
     for copy in round_yz:
         copy.wait_recv()
     vort[0, pl.ds(0, 16, stride=16), :] -= hy[2, 0, 0]
@@ -514,20 +572,16 @@
     own = parts[0:24] + parts[24:48] + parts[48:72]
     for d in range(3):
         tiles[0, :, 512 * d : 512 * d + 512] = own[8 * d : 8 * d + 8]
-    row8, lane8 = iota((8, 128), 0), iota((8, 128), 1)
-    label = jnp.zeros((8, 128), jnp.int32)
-    for t in range(8):
-        both = jnp.where(lane8 < 64, slot_ref[0, 0, 0, t], element_ref[0, 0, 0, t])
-        label = jnp.where(row8 == t, both, label)
-    tiles[0, :, 1536:1664] = label.astype(F32)
-
-    down = [
-        (k, send(tiles.at[0], tiles.at[k], tile_send.at[k - 1], tile_recv.at[k - 1], at_zh(k)))
-        for k in sorted(range(1, zh_count), key=lambda k: -min(k, zh_count - k))
-    ]
-    down.sort(key=lambda item: item[0])
+    down = {}
+    for part in range(PARTS):
+        block = slice(part * TILE_LANES // PARTS, (part + 1) * TILE_LANES // PARTS)
+        for k in sorted(range(1, zh_count), key=lambda k: -min(k, zh_count - k)):
+            i = part * tile_sends + k - 1
+            down[part, k] = send(
+                tiles.at[0, :, block], tiles.at[k, :, block], tile_send.at[i], tile_recv.at[i],
+                at_zh(k),
+            )
     across = []
-    slots = 4 * x_count
     place = iota((slots, 128), 0)
     peer = zh * x_count + lax.rem(xi + place // 4, x_count)
 
@@ -537,57 +591,54 @@
 
     wanted, wanted_after, wanted_before = slot_of(0), slot_of(1), slot_of(-1)
 
-    def pass_on(k):
-        marks = tiles[k, :, 1536:1664]
+    def pass_on(part, k):
+        marks = labels[0, k]
         named = jnp.where(lane8 < 64, marks, pltpu.roll(marks, 64, 1))
         named = [jnp.broadcast_to(named[t : t + 1], (slots, 128)) for t in range(8)]
 
-        def pick(hits, value, block):
+        def pick(hits, value):
             chosen = jnp.zeros((slots, 128), F32)
             for t in range(8):
                 row = jnp.broadcast_to(value[t : t + 1], (slots, 128))
                 chosen = jnp.where(hits[t], row, chosen)
+            return chosen
+
+        def keep(chosen, block):
             full[k * slots : k * slots + 4, block] = chosen[0:4]
             for j in range(1, x_count):
                 parcel[k, j - 1, :, block] = chosen[4 * j : 4 * j + 4]
 
         hits = [n == wanted for n in named]
-        for first in range(0, TILE_LANES, 128):
-            block = slice(first, first + 128)
-            pick(hits, tiles[k, :, block], block)
-        low_face = jnp.where(lane8 < 64, tiles[k, :, 0:128], marks)
-        pick([n == wanted_after for n in named], low_face, slice(1664, 1792))
-        high_face = jnp.where(lane8 < 64, pltpu.roll(marks, 64, 1), tiles[k, :, 384:512])
-        pick([n == wanted_before for n in named], high_face, slice(1792, 1920))
-        for j in range(1, x_count):
-            i = zh_count - 1 + k * (x_count - 1) + j - 1
-            across.append(
-                send(
-                    parcel.at[k, j - 1], arrived.at[k, j - 1], tile_send.at[i], tile_recv.at[i],
-                    at_xi(j),
-                )
+        start, stop = (n * TILE_LANES // PARTS for n in (part, part + 1))
+        for first in range(start, stop, 128):
+            value = pick(hits, tiles[k, :, first : first + 128])
+            keep(value, slice(first + 128, first + 256))
+        if part == 0:
+            shared = jnp.where(lane8 < 64, tiles[k, :, 0:128], tiles[k, :, 384:512])
+            after = pick([n == wanted_after for n in named], shared)
+            before = pick([n == wanted_before for n in named], shared)
+            keep(jnp.where(iota((slots, 128), 1) < 64, after, before), slice(0, 128))
+        block = slice(start + 128 if part else 0, stop + 128)
+        for j in sorted(range(1, x_count), key=lambda j: -min(j, x_count - j)):
+            i = part * tile_sends + zh_count - 1 + k * (x_count - 1) + j - 1
+            copy = send(
+                parcel.at[k, j - 1, :, block], arrived.at[k, j - 1, :, block], tile_send.at[i],
+                tile_recv.at[i], at_xi(j),
             )
-
-    pass_on(0)
-
-    for k in sorted(range(1, zh_count), key=lambda k: min(k, zh_count - k)):
-        down[k - 1][1].wait_recv()
-        pass_on(k)
-    for i, copy in enumerate(across):
+            across.append((k, j, block, copy))
+
+    for part in range(PARTS):
+        pass_on(part, 0)
+    for part in range(PARTS):
+        for k in sorted(range(1, zh_count), key=lambda k: min(k, zh_count - k)):
+            down[part, k].wait_recv()
+            pass_on(part, k)
+    for k, j, block, copy in across:
         copy.wait_recv()
-    for k in range(zh_count):
-        for j in range(1, x_count):
-            top = k * slots + 4 * j
-            full[top : top + 4, :] = arrived[k, j - 1]
-    count = zh_count * slots
-    lanes = iota((count, 128), 1)
-    element = (lanes - 64).astype(F32)
-    picking = jnp.where(full[:, 1536:1664] == element, 1.0, 0.0)
-    picking = jnp.concatenate([picking, picking], axis=0)
-    picking = jnp.transpose(picking)[64:96].astype(BF16)
-
+        top = k * slots + 4 * j
+        full[top : top + 4, block] = arrived[k, j - 1, :, block]
     def pick_source(d):
-        high, low = halves(full[:, 512 * d : 512 * d + 512])
+        high, low = halves(full[:, 512 * d + 128 : 512 * d + 640])
         parts = jnp.concatenate([high, low], axis=0).astype(BF16)
         both = jnp.dot(picking, parts, preferred_element_type=F32)
         q1[1 + d] = -source_gain * sound_step * both
@@ -619,19 +670,8 @@
         block = slice(128 * j, 128 * j + 128)
         chars[0, 0, j] = -q1[1, :, block]
         chars[1, 0, j] = q1[1, :, block]
-    after, before = full[:, 1664:1792], full[:, 1792:1920]
-    picking_2 = jnp.concatenate(
-        [
-            jnp.where((lanes >= 64) & (after == element), 1.0, 0.0),
-            jnp.where((lanes < 64) & (before == element + 80.0), 1.0, 0.0),
-        ],
-        axis=0,
-    )
-    if 2 * count < 128:
-        picking_2 = jnp.concatenate([picking_2, jnp.zeros((128 - 2 * count, 128), F32)], axis=0)
-    picking_2 = jnp.transpose(picking_2)[:, 0 : 2 * count]
-    picking_2 = jnp.concatenate([picking_2[64:80], picking_2[0:16]], axis=0).astype(BF16)
-    high, low = halves(jnp.concatenate([after, before], axis=0))
+    faces = full[:, 0:128]
+    high, low = halves(jnp.concatenate([faces, faces], axis=0))
     sides = jnp.dot(picking_2, high.astype(BF16), preferred_element_type=F32)
     sides += jnp.dot(picking_2, low.astype(BF16), preferred_element_type=F32)
     ax[2, 0] = source_gain * sound_step * sides[0:16]
@@ -639,9 +679,7 @@
     rates(q1, q0, 0.5 * sound_step, lambda c: n0[c] + (q1[c] if c else 0.0), [None, None] + faces_2, 2, False)
     for i in range(32):
         c, part = i // 8, i % 8
-        stage[i] = q0[c, 4 * part : 4 * part + 4, :]
-    stores.append(pltpu.make_async_copy(stage, sound_out, out_sem.at[3]))
-    stores[-1].start()
+        sound_out[i] = q0[c, 4 * part : 4 * part + 4, :]
     for copy in pending:
         copy.wait_send()
     for store in stores:
@@ -661,6 +699,7 @@
     x_count = 4 if gx_count == 16 else 2
     zh_count = gx_count // x_count
     tile_sends = (zh_count - 1) + zh_count * (x_count - 1)
+    label_sends = zh_count + x_count - 2
     consts = tables()
 
     def on_device(density, momentum, energy, acoustic, tile_slot, tile_element):
@@ -681,6 +720,7 @@
             vmem((zh_count, x_count - 1, 4, PARCEL_LANES), F32),
             vmem((zh_count, x_count - 1, 4, PARCEL_LANES), F32),
             vmem((4 * gx_count, PARCEL_LANES), F32),
+            vmem((x_count, zh_count, 8, 128), F32), vmem((3, 4 * gx_count, 128), F32),
             vmem((3, 2, 5, 16, 128), F32), vmem((3, 2, 5, 16, 128), F32),
             vmem((3, 2, 5, 16, 128), F32), vmem((3, 2, 5, 16, 128), F32),
             vmem((3, 5, 16, 128), F32),
@@ -691,17 +731,19 @@
             vmem((512, 512), BF16), vmem((512, 512), BF16), vmem((256, 256), BF16),
             vmem((256, 256), BF16), vmem((256, 256), BF16), vmem((256, 256), BF16),
             vmem((512, 512), BF16),
-            pltpu.SemaphoreType.DMA((11,)), pltpu.SemaphoreType.DMA((4,)),
+            pltpu.SemaphoreType.DMA((11,)), pltpu.SemaphoreType.DMA((3,)),
             pltpu.SemaphoreType.DMA((3, 6)), pltpu.SemaphoreType.DMA((3, 6)),
             pltpu.SemaphoreType.DMA((3, 6)), pltpu.SemaphoreType.DMA((3, 6)),
-            pltpu.SemaphoreType.DMA((tile_sends,)), pltpu.SemaphoreType.DMA((tile_sends,)),
+            pltpu.SemaphoreType.DMA((PARTS * tile_sends,)),
+            pltpu.SemaphoreType.DMA((PARTS * tile_sends,)),
+            pltpu.SemaphoreType.DMA((label_sends,)), pltpu.SemaphoreType.DMA((label_sends,)),
         ]
         held_shape = tuple(pltpu.VMEM(o.shape, F32) for o in out_shape)
         outs = pl.pallas_call(
             functools.partial(kernel, zh_count, x_count, gy_count, gz_count),
             out_shape=held_shape,
             in_specs=[anywhere] * 4 + [scalars] * 2 + [anywhere] * 7,
-            out_specs=[anywhere] * 4,
+            out_specs=[anywhere] * 3 + [pl.BlockSpec(memory_space=pltpu.VMEM)],
             scratch_shapes=scratch,
             compiler_params=pltpu.CompilerParams(
                 collective_id=0, has_side_effects=True, vmem_limit_bytes=57 * 2**20

time: 45.5 us -> 45.2 us (level)
  no operation moved by 1% of the time
where the time goes in v4:
time: 45.2 us; the launch traced here: 45.1 us
  Pallas kernels  44.4 us (98%)
  between operations  0.64 us (1%)
    pallas_call x1, Pallas kernels, on_device(): pl.pallas_call(functools.partial(kernel, zh_count, x_count, gy_count, gz_...  43.5 us
    pallas_call x1, Pallas kernels, on_device(): pl.pallas_call(hand_over, out_shape=out_shape, in_specs=[anywhere] * 4, o...  0.96 us

profile of v4, /device:TPU:2, one launch (start us, length us, event | category | flops | bytes accessed | tf_op | source)
XLA Modules:
  0.0 45.1 jit_solution(743094907499302349)
XLA Ops:
  0.6 43.5 %shard_map.156 = (f32[256,128]{1,0:T(8,128)S(1)}, f32[3,256,128]{2,1,0:T(8,128)S(1)}, f32[256,128]{1,0:T(8,128)S(1)}, f32[32,4,512]{2,1,0:T(4,128)S(1)}) custom-call(f32[256,128]{1,0:T(8,128)} %bitcast.12, f32[3,256,128]{2,1,0:T(8,128)} %bitcast.8, f32[256,128]{1,0:T(8,128)} %bitcast.13, f32[32,4,512]{2,1,0:T(4,128)} %bitcast.10, s32[1,1,1,8]{3,2,1,0:T(1,128)} %slot_ref.1, ...), custom_call_target="tpu_custom_call" | custom-call | flops 1000000000 | bytes 4194304 | tf_op jit(solution)/shard_map/pallas_call | solution.py:742
  44.1 1.0 %shard_map.157 = (f32[256,128]{1,0:T(8,128)}, f32[3,256,128]{2,1,0:T(8,128)}, f32[256,128]{1,0:T(8,128)}, f32[32,4,512]{2,1,0:T(4,128)}) custom-call(f32[256,128]{1,0:T(8,128)S(1)} %get-tuple-element.12.refs_0_, f32[3,256,128]{2,1,0:T(8,128)S(1)} %get-tuple-element.13.refs_1_, f32[256,128]{1,0:T(8,128)S(1)} %get-tuple-element.14.refs_2_, ...), custom_call_target="tpu_custom_call" | custom-call | tf_op jit(solution)/shard_map/pallas_call | solution.py:759

commit v5 on v4

--- a/solution.py
+++ b/solution.py
@@ -476,7 +476,6 @@
         return carry
 
     lax.fori_loop(0, 16, curl, 0)
-    rates(q1, n0, 0.5 * sound_step, lambda c: 0.5 * (q0[c] + q1[c]), faces_1, 1, True)
 
     slots = 4 * x_count
     count = zh_count * slots
@@ -633,6 +632,7 @@
         for k in sorted(range(1, zh_count), key=lambda k: min(k, zh_count - k)):
             down[part, k].wait_recv()
             pass_on(part, k)
+    rates(q1, n0, 0.5 * sound_step, lambda c: 0.5 * (q0[c] + q1[c]), faces_1, 1, True)
     for k, j, block, copy in across:
         copy.wait_recv()
         top = k * slots + 4 * j

time: 45.2 us -> 45.2 us (level)
  no operation moved by 1% of the time
where the time goes in v5:
time: 45.2 us; the launch traced here: 45.1 us
  Pallas kernels  44.4 us (98%)
  between operations  0.64 us (1%)
    pallas_call x1, Pallas kernels, on_device(): pl.pallas_call(functools.partial(kernel, zh_count, x_count, gy_count, gz_...  43.5 us
    pallas_call x1, Pallas kernels, on_device(): pl.pallas_call(hand_over, out_shape=out_shape, in_specs=[anywhere] * 4, o...  0.96 us

profile of v5, /device:TPU:2, one launch (start us, length us, event | category | flops | bytes accessed | tf_op | source)
XLA Modules:
  0.0 45.1 jit_solution(16557750469411483696)
XLA Ops:
  0.6 43.5 %shard_map.156 = (f32[256,128]{1,0:T(8,128)S(1)}, f32[3,256,128]{2,1,0:T(8,128)S(1)}, f32[256,128]{1,0:T(8,128)S(1)}, f32[32,4,512]{2,1,0:T(4,128)S(1)}) custom-call(f32[256,128]{1,0:T(8,128)} %bitcast.12, f32[3,256,128]{2,1,0:T(8,128)} %bitcast.8, f32[256,128]{1,0:T(8,128)} %bitcast.13, f32[32,4,512]{2,1,0:T(4,128)} %bitcast.10, s32[1,1,1,8]{3,2,1,0:T(1,128)} %slot_ref.1, ...), custom_call_target="tpu_custom_call" | custom-call | flops 1000000000 | bytes 4194304 | tf_op jit(solution)/shard_map/pallas_call | solution.py:742
  44.1 1.0 %shard_map.157 = (f32[256,128]{1,0:T(8,128)}, f32[3,256,128]{2,1,0:T(8,128)}, f32[256,128]{1,0:T(8,128)}, f32[32,4,512]{2,1,0:T(4,128)}) custom-call(f32[256,128]{1,0:T(8,128)S(1)} %get-tuple-element.12.refs_0_, f32[3,256,128]{2,1,0:T(8,128)S(1)} %get-tuple-element.13.refs_1_, f32[256,128]{1,0:T(8,128)S(1)} %get-tuple-element.14.refs_2_, ...), custom_call_target="tpu_custom_call" | custom-call | tf_op jit(solution)/shard_map/pallas_call | solution.py:759
